TPU v7x, 32 devices: a whole 2x2x4 slice. The times are simulated.
32 devices in a mesh: sec: 4 (over y, core), row: 8 (over z, x).
Axes of the slice: x: 2, y: 2, z: 4, core: 2. Of those that a mesh axis runs over, the one named last changes fastest.
Arguments:
- env_in: bfloat16 [32, 4, 2, 256, 512], P('row', 'sec'), may hold values from -6 to 6
- ket_mps: bfloat16 [4, 4, 2, 512, 512], P(None, 'sec'), may hold values from -0.25 to 0.25
- bra_mps: bfloat16 [4, 4, 2, 256, 256], P(None, 'sec'), may hold values from -0.375 to 0.375
- ket_sizes: int32 [4, 2], replicated, may hold values from 64 to 512, as said below
- bra_sizes: int32 [4, 2], replicated, may hold values from 64 to 256, as said below
- entries: int32 [32, 8, 3], P('row'), may hold values from 0 to 31, as said below
- coeffs: float32 [32, 8], P('row'), may hold values from -3 to 3
Outputs:
- env_out: bfloat16 [32, 4, 2, 256, 512], P('row', 'sec')
Inputs may be any that keep to these rules, and one draw needn't show every extreme that they name: `ket_sizes`: each ket sector size is at least 64 and at most 512; one sector has exactly 512. `bra_sizes`: each bra sector size is at least 64 and at most 256; one sector has exactly 256. `entries`: every entry (wo, sp, s) of input channel wi conserves charge: c(wo) = c(wi) + n(sp) - n(s); sp and s lie in 0 to 3.
All inputs are finite; a program needn't handle non-finite values.
Results may differ from a plain program's by a relative error of at most 0.014.
Values may be sent and summed in bfloat16 or wider, within the bound.
A program may use at most 128 MiB of HBM per device.

v0:
```python
import jax
import jax.numpy as jnp
from jax import lax
from jax.sharding import PartitionSpec as P

EPW = 8


def passed_along(value, axis, steps):
    count = lax.axis_size(axis)
    first, last = (max(0, -steps), min(count, count - steps))
    return lax.ppermute(value, axis, [(source, source + steps) for source in range(first, last)])


def extended(cells, sides, width):
    for axis, dim in sides:
        count = lax.axis_size(axis)
        ends = count - 1
        head = lax.slice_in_dim(cells, 0, width, axis=dim)
        tail = lax.slice_in_dim(cells, cells.shape[dim] - width, cells.shape[dim], axis=dim)
        cells = jnp.concatenate(
            [
                lax.ppermute(tail, axis, [(i, (i + 1) % count) for i in range(ends)]),
                cells,
                lax.ppermute(head, axis, [((i + 1) % count, i) for i in range(ends)]),
            ],
            axis=dim,
        )
    return cells


def channel_charge(channel):
    klass = channel % 9
    return (klass % 3 - 1, klass // 3 - 1)


def keep_block(block, rows, cols):
    keep_rows = lax.broadcasted_iota(jnp.int32, block.shape, block.ndim - 2) < rows[..., None, None]
    keep_cols = lax.broadcasted_iota(jnp.int32, block.shape, block.ndim - 1) < cols[..., None, None]
    return jnp.where(keep_rows & keep_cols, block, jnp.zeros_like(block))


def body(env_in, ket_mps, bra_mps, ket_sizes, bra_sizes, entries, coeffs):
    chans, _, sec_b, bra_w, ket_w = env_in.shape
    my_a = lax.axis_index("sec")
    first_w = lax.axis_index("row") * chans
    ket_ext = jnp.pad(ket_sizes, 2)
    bra_ext = jnp.pad(bra_sizes, 2)
    zero = jnp.zeros((), jnp.int32)

    def sizes_at(ext, shift_a, shift_b):
        return lax.dynamic_slice(ext, (my_a + shift_a + 2, shift_b + 2), (1, sec_b))

    lower_env, lower_ket = passed_along((env_in, ket_mps[1::2]), "sec", 1)
    env_two = jnp.pad(
        jnp.concatenate([lower_env, env_in], axis=1), ((0, 0), (0, 0), (1, 0), (0, 0), (0, 0))
    )
    ket_all = jnp.pad(
        jnp.concatenate([ket_mps, lower_ket], axis=0), ((0, 0), (0, 0), (1, 0), (0, 0), (0, 0))
    )
    bra_rim = extended(bra_mps, (("sec", 1),), 1)
    bra_all = jnp.pad(bra_rim, ((0, 0), (0, 0), (1, 1), (0, 0), (0, 0)))

    def entry_term(item):
        chan = item // EPW
        slot = item % EPW
        out_w = entries[chan, slot, 0]
        phys_bra = entries[chan, slot, 1]
        phys_ket = entries[chan, slot, 2]
        value = coeffs[chan, slot]
        up_a = phys_ket % 2
        up_b = phys_ket // 2
        in_a, in_b = channel_charge(first_w + chan)
        out_a, out_b = channel_charge(out_w)
        env_blk = lax.dynamic_slice(
            env_two, (chan, 1 - up_a, 1 - up_b, zero, zero), (1, 1, sec_b, bra_w, ket_w)
        )[0]
        ket_index = jnp.where(up_a == 0, phys_ket, 4 + phys_ket // 2)
        ket_blk = lax.dynamic_slice(
            ket_all, (ket_index, zero, 1 - up_b, zero, zero), (1, 1, sec_b, ket_w, ket_w)
        )[0]
        bra_blk = lax.dynamic_slice(
            bra_all, (phys_bra, 1 + out_a, 1 + out_b, zero, zero), (1, 1, sec_b, bra_w, bra_w)
        )[0]
        ket_src = sizes_at(ket_ext, -up_a, -up_b)
        env_blk = keep_block(env_blk, sizes_at(bra_ext, in_a - up_a, in_b - up_b), ket_src)
        ket_blk = keep_block(ket_blk, ket_src, sizes_at(ket_ext, zero, zero))
        bra_blk = keep_block(
            bra_blk,
            sizes_at(bra_ext, out_a - phys_bra % 2, out_b - phys_bra // 2),
            sizes_at(bra_ext, out_a, out_b),
        )
        half = jnp.einsum(
            "abik,abkl->abil", env_blk, ket_blk, preferred_element_type=jnp.float32
        ).astype(jnp.bfloat16)
        return value * jnp.einsum(
            "abij,abil->abjl", bra_blk, half, preferred_element_type=jnp.float32
        )

    count = chans * lax.axis_size("row")

    def step(item, partial_value):
        out_w = entries[item // EPW, item % EPW, 0]
        inside = (out_w >= zero) & (out_w < zero + count)

        def add_term(acc):
            where_at = (out_w, zero, zero, zero, zero)
            old = lax.dynamic_slice(acc, where_at, (1, 1, sec_b, bra_w, ket_w))
            return lax.dynamic_update_slice(acc, old + entry_term(item)[None], where_at)

        return lax.cond(inside, add_term, lambda acc: acc, partial_value)

    return lax.psum_scatter(
        lax.fori_loop(
            0, chans * EPW, step, jnp.zeros((count, 1, sec_b, bra_w, ket_w), jnp.float32)
        ).astype(jnp.bfloat16),
        "row",
        scatter_dimension=0,
        tiled=True,
    )


def solution(mesh):
    placed = (
        P("row", "sec", None, None, None),
        P(None, "sec", None, None, None),
        P(None, "sec", None, None, None),
        P(),
        P(),
        P("row", None, None),
        P("row", None),
    )
    return jax.shard_map(
        body,
        mesh=mesh,
        in_specs=placed,
        out_specs=P("row", "sec", None, None, None),
        check_vma=False,
    )
```

profile of v0, /device:TPU:30, one launch (start us, length us, event | category | flops | bytes accessed | tf_op | source)
XLA Modules:
  0.0 988.8 jit_solution(1863612649197620921)
XLA Ops:
  30.3 16.4 %collective-permute-done.3 = bf16[2,1,2,512,512]{4,3,2,1,0:T(8,128)(2,1)} collective-permute-done((bf16[2,1,2,512,512]{4,3,2,1,0:T(8,128)(2,1)}, bf16[2,1,2,512,512]{4,3,2,1,0:T(8,128)(2,1)}, u32[]{:S(2)}, u32[]{:S(2)}) %collective-permute-start.3) | collective-permute-done | bytes 2097184 | tf_op jit(solution)/shard_map/ppermute | solution.py:12
  52.4 16.7 %collective-permute-done.2 = bf16[4,1,2,256,512]{4,3,2,1,0:T(8,128)(2,1)S(1)} collective-permute-done((bf16[4,1,2,256,512]{4,3,2,1,0:T(8,128)(2,1)}, bf16[4,1,2,256,512]{4,3,2,1,0:T(8,128)(2,1)S(1)}, u32[]{:S(2)}, u32[]{:S(2)}) %collective-permute-start.2) | collective-permute-done | bytes 2097184 | tf_op jit(solution)/shard_map/ppermute | solution.py:12
  84.3 599.1 %while.18 = (s32[]{:T(128)}, f32[32,1,2,256,512]{4,3,2,1,0:T(8,128)}, s32[4,8,3]{1,0,2:T(4,128)}, f32[4,8]{1,0:T(4,128)}, s32[]{:T(128)}, /*index=5*/s32[8,6]{1,...) while((s32[]{:T(128)}, ...), condition=%wide.region_3.4_spmd, body=%wide.region_0.3_spmd.sunk | while | flops 407109824 | bytes 3942862 | solution.py:114
  86.8 16.2 %conditional.2 = (f32[32,1,2,256,512]{4,3,2,1,0:T(8,128)}) conditional(s32[]{:T(128)} %convert_element_type.28, f32[32,1,2,256,512]{4,3,2,1,0:T(8,128)} %get-tuple-element.440, (s32[]{:T(128)}, f32[32,1,2,256,512]{4,3,2,1,0:T(8,128)}, s32[]{:T(128)}, f32[4,8]{1,0:T(4,128)}, s32[4,8,3]{1,0,2:T(4,128)}, /*index=5*/s32[]{:T(128)}, s32[8,6]{1,0:T(8,128)S(1)}, ...), branch_computations={%region_1.1_spmd, %region_2.2_spmd} | conditional | flops 407109792 | bytes 3942368 | solution.py:111
  105.6 16.2 %conditional.2 = (f32[32,1,2,256,512]{4,3,2,1,0:T(8,128)}) conditional(s32[]{:T(128)} %convert_element_type.28, f32[32,1,2,256,512]{4,3,2,1,0:T(8,128)} %get-tuple-element.440, (s32[]{:T(128)}, f32[32,1,2,256,512]{4,3,2,1,0:T(8,128)}, s32[]{:T(128)}, f32[4,8]{1,0:T(4,128)}, s32[4,8,3]{1,0,2:T(4,128)}, /*index=5*/s32[]{:T(128)}, s32[8,6]{1,0:T(8,128)S(1)}, ...), branch_computations={%region_1.1_spmd, %region_2.2_spmd} | conditional | flops 407109792 | bytes 3942368 | solution.py:111
  143.0 16.2 %conditional.2 = (f32[32,1,2,256,512]{4,3,2,1,0:T(8,128)}) conditional(s32[]{:T(128)} %convert_element_type.28, f32[32,1,2,256,512]{4,3,2,1,0:T(8,128)} %get-tuple-element.440, (s32[]{:T(128)}, f32[32,1,2,256,512]{4,3,2,1,0:T(8,128)}, s32[]{:T(128)}, f32[4,8]{1,0:T(4,128)}, s32[4,8,3]{1,0,2:T(4,128)}, /*index=5*/s32[]{:T(128)}, s32[8,6]{1,0:T(8,128)S(1)}, ...), branch_computations={%region_1.1_spmd, %region_2.2_spmd} | conditional | flops 407109792 | bytes 3942368 | solution.py:111
  180.4 16.2 %conditional.2 = (f32[32,1,2,256,512]{4,3,2,1,0:T(8,128)}) conditional(s32[]{:T(128)} %convert_element_type.28, f32[32,1,2,256,512]{4,3,2,1,0:T(8,128)} %get-tuple-element.440, (s32[]{:T(128)}, f32[32,1,2,256,512]{4,3,2,1,0:T(8,128)}, s32[]{:T(128)}, f32[4,8]{1,0:T(4,128)}, s32[4,8,3]{1,0,2:T(4,128)}, /*index=5*/s32[]{:T(128)}, s32[8,6]{1,0:T(8,128)S(1)}, ...), branch_computations={%region_1.1_spmd, %region_2.2_spmd} | conditional | flops 407109792 | bytes 3942368 | solution.py:111
  199.1 16.2 %conditional.2 = (f32[32,1,2,256,512]{4,3,2,1,0:T(8,128)}) conditional(s32[]{:T(128)} %convert_element_type.28, f32[32,1,2,256,512]{4,3,2,1,0:T(8,128)} %get-tuple-element.440, (s32[]{:T(128)}, f32[32,1,2,256,512]{4,3,2,1,0:T(8,128)}, s32[]{:T(128)}, f32[4,8]{1,0:T(4,128)}, s32[4,8,3]{1,0,2:T(4,128)}, /*index=5*/s32[]{:T(128)}, s32[8,6]{1,0:T(8,128)S(1)}, ...), branch_computations={%region_1.1_spmd, %region_2.2_spmd} | conditional | flops 407109792 | bytes 3942368 | solution.py:111
  292.7 16.2 %conditional.2 = (f32[32,1,2,256,512]{4,3,2,1,0:T(8,128)}) conditional(s32[]{:T(128)} %convert_element_type.28, f32[32,1,2,256,512]{4,3,2,1,0:T(8,128)} %get-tuple-element.440, (s32[]{:T(128)}, f32[32,1,2,256,512]{4,3,2,1,0:T(8,128)}, s32[]{:T(128)}, f32[4,8]{1,0:T(4,128)}, s32[4,8,3]{1,0,2:T(4,128)}, /*index=5*/s32[]{:T(128)}, s32[8,6]{1,0:T(8,128)S(1)}, ...), branch_computations={%region_1.1_spmd, %region_2.2_spmd} | conditional | flops 407109792 | bytes 3942368 | solution.py:111
  367.6 16.2 %conditional.2 = (f32[32,1,2,256,512]{4,3,2,1,0:T(8,128)}) conditional(s32[]{:T(128)} %convert_element_type.28, f32[32,1,2,256,512]{4,3,2,1,0:T(8,128)} %get-tuple-element.440, (s32[]{:T(128)}, f32[32,1,2,256,512]{4,3,2,1,0:T(8,128)}, s32[]{:T(128)}, f32[4,8]{1,0:T(4,128)}, s32[4,8,3]{1,0,2:T(4,128)}, /*index=5*/s32[]{:T(128)}, s32[8,6]{1,0:T(8,128)S(1)}, ...), branch_computations={%region_1.1_spmd, %region_2.2_spmd} | conditional | flops 407109792 | bytes 3942368 | solution.py:111
  386.3 16.2 %conditional.2 = (f32[32,1,2,256,512]{4,3,2,1,0:T(8,128)}) conditional(s32[]{:T(128)} %convert_element_type.28, f32[32,1,2,256,512]{4,3,2,1,0:T(8,128)} %get-tuple-element.440, (s32[]{:T(128)}, f32[32,1,2,256,512]{4,3,2,1,0:T(8,128)}, s32[]{:T(128)}, f32[4,8]{1,0:T(4,128)}, s32[4,8,3]{1,0,2:T(4,128)}, /*index=5*/s32[]{:T(128)}, s32[8,6]{1,0:T(8,128)S(1)}, ...), branch_computations={%region_1.1_spmd, %region_2.2_spmd} | conditional | flops 407109792 | bytes 3942368 | solution.py:111
  423.7 16.2 %conditional.2 = (f32[32,1,2,256,512]{4,3,2,1,0:T(8,128)}) conditional(s32[]{:T(128)} %convert_element_type.28, f32[32,1,2,256,512]{4,3,2,1,0:T(8,128)} %get-tuple-element.440, (s32[]{:T(128)}, f32[32,1,2,256,512]{4,3,2,1,0:T(8,128)}, s32[]{:T(128)}, f32[4,8]{1,0:T(4,128)}, s32[4,8,3]{1,0,2:T(4,128)}, /*index=5*/s32[]{:T(128)}, s32[8,6]{1,0:T(8,128)S(1)}, ...), branch_computations={%region_1.1_spmd, %region_2.2_spmd} | conditional | flops 407109792 | bytes 3942368 | solution.py:111
  461.1 16.2 %conditional.2 = (f32[32,1,2,256,512]{4,3,2,1,0:T(8,128)}) conditional(s32[]{:T(128)} %convert_element_type.28, f32[32,1,2,256,512]{4,3,2,1,0:T(8,128)} %get-tuple-element.440, (s32[]{:T(128)}, f32[32,1,2,256,512]{4,3,2,1,0:T(8,128)}, s32[]{:T(128)}, f32[4,8]{1,0:T(4,128)}, s32[4,8,3]{1,0,2:T(4,128)}, /*index=5*/s32[]{:T(128)}, s32[8,6]{1,0:T(8,128)S(1)}, ...), branch_computations={%region_1.1_spmd, %region_2.2_spmd} | conditional | flops 407109792 | bytes 3942368 | solution.py:111
  479.9 16.2 %conditional.2 = (f32[32,1,2,256,512]{4,3,2,1,0:T(8,128)}) conditional(s32[]{:T(128)} %convert_element_type.28, f32[32,1,2,256,512]{4,3,2,1,0:T(8,128)} %get-tuple-element.440, (s32[]{:T(128)}, f32[32,1,2,256,512]{4,3,2,1,0:T(8,128)}, s32[]{:T(128)}, f32[4,8]{1,0:T(4,128)}, s32[4,8,3]{1,0,2:T(4,128)}, /*index=5*/s32[]{:T(128)}, s32[8,6]{1,0:T(8,128)S(1)}, ...), branch_computations={%region_1.1_spmd, %region_2.2_spmd} | conditional | flops 407109792 | bytes 3942368 | solution.py:111
  498.7 16.2 %conditional.2 = (f32[32,1,2,256,512]{4,3,2,1,0:T(8,128)}) conditional(s32[]{:T(128)} %convert_element_type.28, f32[32,1,2,256,512]{4,3,2,1,0:T(8,128)} %get-tuple-element.440, (s32[]{:T(128)}, f32[32,1,2,256,512]{4,3,2,1,0:T(8,128)}, s32[]{:T(128)}, f32[4,8]{1,0:T(4,128)}, s32[4,8,3]{1,0,2:T(4,128)}, /*index=5*/s32[]{:T(128)}, s32[8,6]{1,0:T(8,128)S(1)}, ...), branch_computations={%region_1.1_spmd, %region_2.2_spmd} | conditional | flops 407109792 | bytes 3942368 | solution.py:111
  517.5 16.2 %conditional.2 = (f32[32,1,2,256,512]{4,3,2,1,0:T(8,128)}) conditional(s32[]{:T(128)} %convert_element_type.28, f32[32,1,2,256,512]{4,3,2,1,0:T(8,128)} %get-tuple-element.440, (s32[]{:T(128)}, f32[32,1,2,256,512]{4,3,2,1,0:T(8,128)}, s32[]{:T(128)}, f32[4,8]{1,0:T(4,128)}, s32[4,8,3]{1,0,2:T(4,128)}, /*index=5*/s32[]{:T(128)}, s32[8,6]{1,0:T(8,128)S(1)}, ...), branch_computations={%region_1.1_spmd, %region_2.2_spmd} | conditional | flops 407109792 | bytes 3942368 | solution.py:111
  536.2 16.2 %conditional.2 = (f32[32,1,2,256,512]{4,3,2,1,0:T(8,128)}) conditional(s32[]{:T(128)} %convert_element_type.28, f32[32,1,2,256,512]{4,3,2,1,0:T(8,128)} %get-tuple-element.440, (s32[]{:T(128)}, f32[32,1,2,256,512]{4,3,2,1,0:T(8,128)}, s32[]{:T(128)}, f32[4,8]{1,0:T(4,128)}, s32[4,8,3]{1,0,2:T(4,128)}, /*index=5*/s32[]{:T(128)}, s32[8,6]{1,0:T(8,128)S(1)}, ...), branch_computations={%region_1.1_spmd, %region_2.2_spmd} | conditional | flops 407109792 | bytes 3942368 | solution.py:111
  554.9 16.2 %conditional.2 = (f32[32,1,2,256,512]{4,3,2,1,0:T(8,128)}) conditional(s32[]{:T(128)} %convert_element_type.28, f32[32,1,2,256,512]{4,3,2,1,0:T(8,128)} %get-tuple-element.440, (s32[]{:T(128)}, f32[32,1,2,256,512]{4,3,2,1,0:T(8,128)}, s32[]{:T(128)}, f32[4,8]{1,0:T(4,128)}, s32[4,8,3]{1,0,2:T(4,128)}, /*index=5*/s32[]{:T(128)}, s32[8,6]{1,0:T(8,128)S(1)}, ...), branch_computations={%region_1.1_spmd, %region_2.2_spmd} | conditional | flops 407109792 | bytes 3942368 | solution.py:111
  611.0 16.2 %conditional.2 = (f32[32,1,2,256,512]{4,3,2,1,0:T(8,128)}) conditional(s32[]{:T(128)} %convert_element_type.28, f32[32,1,2,256,512]{4,3,2,1,0:T(8,128)} %get-tuple-element.440, (s32[]{:T(128)}, f32[32,1,2,256,512]{4,3,2,1,0:T(8,128)}, s32[]{:T(128)}, f32[4,8]{1,0:T(4,128)}, s32[4,8,3]{1,0,2:T(4,128)}, /*index=5*/s32[]{:T(128)}, s32[8,6]{1,0:T(8,128)S(1)}, ...), branch_computations={%region_1.1_spmd, %region_2.2_spmd} | conditional | flops 407109792 | bytes 3942368 | solution.py:111
  629.8 16.2 %conditional.2 = (f32[32,1,2,256,512]{4,3,2,1,0:T(8,128)}) conditional(s32[]{:T(128)} %convert_element_type.28, f32[32,1,2,256,512]{4,3,2,1,0:T(8,128)} %get-tuple-element.440, (s32[]{:T(128)}, f32[32,1,2,256,512]{4,3,2,1,0:T(8,128)}, s32[]{:T(128)}, f32[4,8]{1,0:T(4,128)}, s32[4,8,3]{1,0,2:T(4,128)}, /*index=5*/s32[]{:T(128)}, s32[8,6]{1,0:T(8,128)S(1)}, ...), branch_computations={%region_1.1_spmd, %region_2.2_spmd} | conditional | flops 407109792 | bytes 3942368 | solution.py:111
  648.5 16.2 %conditional.2 = (f32[32,1,2,256,512]{4,3,2,1,0:T(8,128)}) conditional(s32[]{:T(128)} %convert_element_type.28, f32[32,1,2,256,512]{4,3,2,1,0:T(8,128)} %get-tuple-element.440, (s32[]{:T(128)}, f32[32,1,2,256,512]{4,3,2,1,0:T(8,128)}, s32[]{:T(128)}, f32[4,8]{1,0:T(4,128)}, s32[4,8,3]{1,0,2:T(4,128)}, /*index=5*/s32[]{:T(128)}, s32[8,6]{1,0:T(8,128)S(1)}, ...), branch_computations={%region_1.1_spmd, %region_2.2_spmd} | conditional | flops 407109792 | bytes 3942368 | solution.py:111
  667.2 16.2 %conditional.2 = (f32[32,1,2,256,512]{4,3,2,1,0:T(8,128)}) conditional(s32[]{:T(128)} %convert_element_type.28, f32[32,1,2,256,512]{4,3,2,1,0:T(8,128)} %get-tuple-element.440, (s32[]{:T(128)}, f32[32,1,2,256,512]{4,3,2,1,0:T(8,128)}, s32[]{:T(128)}, f32[4,8]{1,0:T(4,128)}, s32[4,8,3]{1,0,2:T(4,128)}, /*index=5*/s32[]{:T(128)}, s32[8,6]{1,0:T(8,128)S(1)}, ...), branch_computations={%region_1.1_spmd, %region_2.2_spmd} | conditional | flops 407109792 | bytes 3942368 | solution.py:111
  683.4 17.3 %convert_element_type.23 = bf16[32,1,2,256,512]{4,3,2,1,0:T(8,128)(2,1)} convert(f32[32,1,2,256,512]{4,3,2,1,0:T(8,128)} %get-tuple-element.319) | non-fusion elementwise | flops 8388608 | bytes 50331648 | tf_op jit(solution)/shard_map/convert_element_type | solution.py:116
  700.7 281.2 %reduce-scatter.2.cloned.1.call-done = bf16[4,1,2,256,512]{4,3,2,1,0:T(8,128)(2,1)} async-done(((bf16[32,1,2,256,512]{4,3,2,1,0:T(8,128)(2,1)}), bf16[4,1,2,256,512]{4,3,2,1,0:T(8,128)(2,1)}) %reduce-scatter.2.cloned.1.call-update) | async-done | bytes 2097168 | tf_op jit(solution)/shard_map/reduce_scatter | solution.py:113
  (199 shorter events, 514.6 us)
Async XLA Ops:
  6.5 14.0 %copy-start.2 = (s32[4,2]{0,1:T(2,128)S(1)}, s32[4,2]{0,1:T(2,128)}, u32[]{:S(2)}) copy-start(s32[4,2]{0,1:T(2,128)} %param.15) | copy-start | bytes 100
  6.5 14.2 %copy-start.3 = (s32[4,2]{0,1:T(2,128)S(1)}, s32[4,2]{0,1:T(2,128)}, u32[]{:S(2)}) copy-start(s32[4,2]{0,1:T(2,128)} %param.14) | copy-start | bytes 100
  6.5 975.4 %reduce-scatter.2.cloned.1.call-start = ((), (), s32[]{:S(2)}) async-start(), calls=%async_computation.1 | async-start | bytes 18874368 | tf_op jit(solution)/shard_map/reduce_scatter | solution.py:113
  8.0 16.2 %collective-permute-start = (bf16[4,1,2,256,256]{3,4,2,1,0:T(8,128)(2,1)S(1)}, bf16[4,1,2,256,256]{3,4,2,1,0:T(8,128)(2,1)}, u32[]{:S(2)}, u32[]{:S(2)}) collective-permute-start(bf16[4,1,2,256,256]{3,4,2,1,0:T(8,128)(2,1)S(1)} %copy.9), channel_id=1, source_target_pairs={{0,8},{8,16},{16,24},{1,9},{9,17},{17,25},{2,10},{10,18},{18,26},{... | collective-permute-start | bytes 3145736 | tf_op jit(solution)/shard_map/ppermute | solution.py:23
  10.0 15.9 %collective-permute-start.1 = (bf16[4,1,2,256,256]{3,4,2,1,0:T(8,128)(2,1)S(1)}, bf16[4,1,2,256,256]{3,4,2,1,0:T(8,128)(2,1)}, u32[]{:S(2)}, u32[]{:S(2)}) collective-permute-start(bf16[4,1,2,256,256]{3,4,2,1,0:T(8,128)(2,1)S(1)} %copy.9), channel_id=1, source_target_pairs={{8,0},{16,8},{24,16},{9,1},{17,9},{25,17},{10,2},{18,10},{26,18},{... | collective-permute-start | bytes 3145736 | tf_op jit(solution)/shard_map/ppermute | solution.py:25
  16.7 30.1 %collective-permute-start.3 = (bf16[2,1,2,512,512]{4,3,2,1,0:T(8,128)(2,1)}, bf16[2,1,2,512,512]{4,3,2,1,0:T(8,128)(2,1)}, u32[]{:S(2)}, u32[]{:S(2)}) collective-permute-start(bf16[2,1,2,512,512]{4,3,2,1,0:T(8,128)(2,1)} %slice.3), channel_id=1, source_target_pairs={{0,8},{8,16},{16,24},{1,9},{9,17},{17,25},{2,10},{10,18},{18,26},{... | collective-permute-start | bytes 6291464 | tf_op jit(solution)/shard_map/ppermute | solution.py:12
  18.6 50.5 %collective-permute-start.2 = (bf16[4,1,2,256,512]{4,3,2,1,0:T(8,128)(2,1)}, bf16[4,1,2,256,512]{4,3,2,1,0:T(8,128)(2,1)S(1)}, u32[]{:S(2)}, u32[]{:S(2)}) collective-permute-start(bf16[4,1,2,256,512]{4,3,2,1,0:T(8,128)(2,1)} %param.11), channel_id=1, source_target_pairs={{0,8},{8,16},{16,24},{1,9},{9,17},{17,25},{2,10},{10,18},{18,26},{... | collective-permute-start | bytes 6291464 | tf_op jit(solution)/shard_map/ppermute | solution.py:12
  20.9 25.8 %copy-start = (bf16[4,1,2,512,512]{4,3,2,1,0:T(8,128)(2,1)S(1)}, bf16[4,1,2,512,512]{4,3,2,1,0:T(8,128)(2,1)}, u32[]{:S(2)}) copy-start(bf16[4,1,2,512,512]{4,3,2,1,0:T(8,128)(2,1)} %param.12) | copy-start | bytes 12582916
  30.3 38.8 %copy-start.1 = (bf16[4,1,2,256,512]{4,3,2,1,0:T(8,128)(2,1)S(1)}, bf16[4,1,2,256,512]{4,3,2,1,0:T(8,128)(2,1)}, u32[]{:S(2)}) copy-start(bf16[4,1,2,256,512]{4,3,2,1,0:T(8,128)(2,1)} %param.11) | copy-start | bytes 6291460
Sparse Core Ops, SparseCore 0:
  700.8 281.0 reduce-scatter.1
where the time goes:
time: 1000 us; the launch traced here: 989 us
  loops' own time  339 us (34%)
  waiting for transfers between devices  319 us (32%)
  local copies, waits for them, and re-layouts  143 us (14%)
  matrix products  133 us (13%)
  other arithmetic  31.2 us (3%)
  between operations  13.5 us (1%)
    another operation x32, loops' own time, step(): return lax.cond(inside, add_term, lambda acc: acc, partial_value)  297 us
    reduce_scatter x1, waiting for transfers between devices, body(): lax.psum_scatter(lax.fori_loop(0, chans * EPW, step, jnp.zeros((count, 1,...  281 us
    dot_general x32, matrix products, entry_term(): jnp.einsum('abij,abil->abjl', bra_blk, half, preferred_element_type=jnp.f...  133 us
    dynamic_slice x32, local copies, waits for them, and re-layouts, entry_term(): out_w = entries[chan, slot, 0]  44 us
    another operation x1, loops' own time, body(): lax.fori_loop(0, chans * EPW, step, jnp.zeros((count, 1, sec_b, bra_w, ke...  41.7 us
    dynamic_slice x32, local copies, waits for them, and re-layouts, step(): out_w = entries[item // EPW, item % EPW, 0]  40.4 us
    dynamic_slice x32, local copies, waits for them, and re-layouts, entry_term(): value = coeffs[chan, slot]  39.6 us
    ppermute x2, waiting for transfers between devices, passed_along(): lax.ppermute(value, axis, [(source, source + steps) for source in range(f...  33.1 us
  transfers between devices with their start and end apart: 5, of which 5 were waited for; matrix products, arithmetic and copies ran while one was open for 1% of the time, Pallas kernels for 0%

commit v1 on v0

v1 whole, which is shorter than its diff:
```python
import functools

import jax
import jax.numpy as jnp
from jax import lax
from jax.experimental import pallas as pl
from jax.experimental.pallas import tpu as pltpu
from jax.sharding import PartitionSpec as P

EPW = 8
Z = 4
DEPTH = 8
MESH = pl.DeviceIdType.MESH


def channel_charge(channel):
    klass = lax.rem(channel, 9)
    return lax.rem(klass, 3) - 1, lax.div(klass, 3) - 1


def ring_pos(row, n):
    wide = n // Z
    z, x = lax.div(row, wide), lax.rem(row, wide)
    t = jnp.where(lax.rem(z, 2) == 0, x - 1, wide - 1 - x)
    return jnp.where(x == 0, Z * (wide - 1) + Z - 1 - z, z * (wide - 1) + t)


def ring_row(pos, n):
    wide = n // Z
    z, t = lax.div(pos, wide - 1), lax.rem(pos, wide - 1)
    x = jnp.where(lax.rem(z, 2) == 0, 1 + t, wide - 1 - t)
    back = Z - 1 - (pos - Z * (wide - 1))
    return jnp.where(pos < Z * (wide - 1), z * wide + x, back * wide)


def gather_kernel(n, chans, sec_a, sec_b, env, bra, info, env_all, bra_all, info_all,
                  send, recv, isend, irecv, bsend, brecv, local):
    a = lax.axis_index("sec")
    row = lax.axis_index("row")
    pos = ring_pos(row, n)
    half = n // 2
    right, left = (ring_row(lax.rem(pos + d, n), n) for d in (1, n - 1))
    blocks = chans * sec_b

    barrier = pltpu.get_barrier_semaphore()
    for other in (right, left):
        pl.semaphore_signal(barrier, inc=1, device_id={"row": other}, device_id_type=MESH)
    for d in (-2, -1, 1, 2):
        @pl.when((a + d >= 0) & (a + d < sec_a))
        def _(d=d):
            pl.semaphore_signal(barrier, inc=1, device_id={"sec": a + d}, device_id_type=MESH)
    count = 2 + jnp.minimum(a, 2) + jnp.minimum(sec_a - 1 - a, 2)
    pl.semaphore_wait(barrier, count)

    def live(source, b):
        c_a, c_b = channel_charge(source * chans + b // sec_b)
        x, y = a + c_a, b % sec_b + c_b
        return (x >= 0) & (x < sec_a) & (y >= 0) & (y < sec_b)

    def source_at(k, way):
        return ring_row(lax.rem(pos + (n - k if way == 0 else k), n), n)

    def block_copy(k, way, b, source):
        src = env.at[b] if k == 1 else env_all.at[source * blocks + b]
        return pltpu.make_async_remote_copy(
            src_ref=src, dst_ref=env_all.at[source * blocks + b],
            send_sem=send.at[k - 1, way, b], recv_sem=recv.at[k - 1, way, b],
            device_id={"row": left if way else right}, device_id_type=MESH)

    def info_copy(k, way, source):
        src = info if k == 1 else info_all.at[source]
        return pltpu.make_async_remote_copy(
            src_ref=src, dst_ref=info_all.at[source],
            send_sem=isend.at[k - 1, way], recv_sem=irecv.at[k - 1, way],
            device_id={"row": left if way else right}, device_id_type=MESH)

    def used(k, way, b):
        return k < half or (b < blocks // 2) == (way == 0)

    def info_used(k, way):
        return k < half or way == 0

    def bra_copies():
        made = []
        for j, (d, slot) in enumerate(((1, 0), (-1, 2), (-2, 3))):
            made.append((d, pltpu.make_async_remote_copy(
                src_ref=bra, dst_ref=bra_all.at[slot],
                send_sem=bsend.at[j], recv_sem=brecv.at[j],
                device_id={"sec": a + d}, device_id_type=MESH)))
        return made

    for way in (0, 1):
        info_copy(1, way, row).start()
    for b in range(blocks):
        @pl.when(live(row, b))
        def _(b=b):
            for way in (0, 1):
                if used(1, way, b):
                    block_copy(1, way, b, row).start()
    for d, copy in bra_copies():
        @pl.when((a + d >= 0) & (a + d < sec_a))
        def _(copy=copy):
            copy.start()
    own = (
        pltpu.make_async_copy(env, env_all.at[pl.ds(row * blocks, blocks)], local.at[0]),
        pltpu.make_async_copy(bra, bra_all.at[1], local.at[1]),
        pltpu.make_async_copy(info, info_all.at[row], local.at[2]),
    )
    for copy in own:
        copy.start()

    for k in range(1, half + 1):
        sources = [source_at(k, way) for way in (0, 1)]
        for way in (0, 1):
            if info_used(k, way):
                info_copy(k, way, sources[way]).wait_recv()
                if k < half and info_used(k + 1, way):
                    info_copy(k + 1, way, sources[way]).start()
        for b in range(blocks):
            for way in (0, 1):
                if used(k, way, b):
                    @pl.when(live(sources[way], b))
                    def _(k=k, way=way, b=b):
                        block_copy(k, way, b, sources[way]).wait_recv()
                        if k < half and used(k + 1, way, b):
                            block_copy(k + 1, way, b, sources[way]).start()

    for k in range(1, half + 1):
        for way in (0, 1):
            source = row if k == 1 else source_at(k - 1, way)
            if info_used(k, way):
                info_copy(k, way, source).wait_send()
            for b in range(blocks):
                if used(k, way, b):
                    @pl.when(live(source, b))
                    def _(k=k, way=way, b=b, source=source):
                        block_copy(k, way, b, source).wait_send()
    for d, copy in bra_copies():
        @pl.when((a + d >= 0) & (a + d < sec_a))
        def _(copy=copy):
            copy.wait_send()

        @pl.when((a - d >= 0) & (a - d < sec_a))
        def _(copy=copy):
            copy.wait_recv()
    for copy in own:
        copy.wait()


def gather(env, bra, info, n, chans, sec_a, sec_b):
    half, blocks = n // 2, chans * sec_b
    anywhere = pl.BlockSpec(memory_space=pl.ANY)
    dma = pltpu.SemaphoreType.DMA
    return pl.pallas_call(
        functools.partial(gather_kernel, n, chans, sec_a, sec_b),
        out_shape=(
            jax.ShapeDtypeStruct((n * blocks,) + env.shape[1:], env.dtype),
            jax.ShapeDtypeStruct((4,) + bra.shape, bra.dtype),
            jax.ShapeDtypeStruct((n,) + info.shape, info.dtype),
        ),
        in_specs=[anywhere] * 3,
        out_specs=(anywhere,) * 3,
        scratch_shapes=[
            dma((half, 2, blocks)), dma((half, 2, blocks)), dma((half, 2)), dma((half, 2)),
            dma((3,)), dma((3,)), dma((3,)),
        ],
        compiler_params=pltpu.CompilerParams(collective_id=0, has_side_effects=True),
        name="gather_row",
    )(env, bra, info)


def terms_kernel(up_a, chans, starts, packed, values, ksz, env, bra, ket, out, buf, t_acc, acc, sems):
    first = starts[up_a * chans * 3]
    last = starts[(up_a + 1) * chans * 3]

    def fetch(j):
        slot = lax.rem(j, DEPTH)
        return pltpu.make_async_copy(env.at[lax.div(packed[j], 32)], buf.at[slot], sems.at[slot])

    for d in range(DEPTH):
        @pl.when(first + d < last)
        def _(d=d):
            fetch(first + d).start()

    acc[...] = jnp.zeros_like(acc)
    cols = lax.broadcasted_iota(jnp.int32, t_acc.shape, 1)

    def channel(i, carry):
        for kind, (up_b, q_b) in enumerate(((0, 0), (0, 1), (1, 0))):
            bucket = (up_a * chans + i) * 3 + kind
            begin, end = starts[bucket], starts[bucket + 1]

            @pl.when(end > begin)
            def _():
                t_acc[...] = jnp.zeros_like(t_acc)

                def item(j, c):
                    fetch(j).wait()
                    b = bra[lax.rem(packed[j], 32)]
                    e = buf[lax.rem(j, DEPTH)]
                    t_acc[...] += values[j] * jnp.dot(b, e, preferred_element_type=jnp.float32)

                    @pl.when(j + DEPTH < last)
                    def _():
                        fetch(j + DEPTH).start()
                    return c

                lax.fori_loop(begin, end, item, 0)
                t = jnp.where(cols < ksz[q_b], t_acc[...], 0.0).astype(jnp.bfloat16)
                k = ket[(up_a + 2 * up_b) * 2 + q_b]
                acc[i * 2 + up_b + q_b] += jnp.dot(t, k, preferred_element_type=jnp.float32)
        for p_b in (0, 1):
            block = acc[i * 2 + p_b]
            out[i * 2 + p_b] = jnp.where(cols < ksz[2 + p_b], block, 0.0).astype(out.dtype)
        return carry

    lax.fori_loop(0, chans, channel, 0)


def terms(up_a, chans, starts, packed, values, ksz, env, bra, ket, dtype):
    rows, cols = env.shape[1:]
    blocks = chans * 2
    smem = pl.BlockSpec(memory_space=pltpu.SMEM)
    vmem = pl.BlockSpec(memory_space=pltpu.VMEM)
    return pl.pallas_call(
        functools.partial(terms_kernel, up_a, chans),
        out_shape=jax.ShapeDtypeStruct((blocks, rows, cols), dtype),
        in_specs=[smem] * 4 + [pl.BlockSpec(memory_space=pl.ANY), vmem, vmem],
        out_specs=vmem,
        scratch_shapes=[
            pltpu.VMEM((DEPTH, rows, cols), env.dtype),
            pltpu.VMEM((rows, cols), jnp.float32),
            pltpu.VMEM((blocks, rows, cols), jnp.float32),
            pltpu.SemaphoreType.DMA((DEPTH,)),
        ],
        compiler_params=pltpu.CompilerParams(vmem_limit_bytes=40 * 1024 * 1024),
        cost_estimate=pl.CostEstimate(flops=5 * 10**9, bytes_accessed=16 * 2**20, transcendentals=0),
        name="terms_up" if up_a else "terms_same",
    )(starts, packed, values, ksz, env, bra, ket)


def body(env_in, ket_mps, bra_mps, ket_sizes, bra_sizes, entries, coeffs):
    chans, _, sec_b, bra_w, ket_w = env_in.shape
    a = lax.axis_index("sec")
    row = lax.axis_index("row")
    sec_a, n = lax.axis_size("sec"), lax.axis_size("row")
    ket_ext = jnp.pad(ket_sizes, 1)
    bra_ext = jnp.pad(bra_sizes, 2)

    def sizes_at(ext, pad, shift_a, shift_b):
        return lax.dynamic_slice(ext, (a + shift_a + pad, jnp.int32(shift_b + pad)), (1, sec_b))[0]

    own = sizes_at(bra_ext, 2, 0, 0)
    src = jnp.stack([sizes_at(bra_ext, 2, -(sp % 2), -(sp // 2)) for sp in range(4)])
    at = jnp.arange(bra_w, dtype=jnp.int32)
    keep = (at[None, None, :, None] < src[:, :, None, None]) & (at < own[None, :, None, None])
    bra = jnp.where(keep, bra_mps[:, 0], jnp.zeros((), bra_mps.dtype)).swapaxes(2, 3)
    bra = bra.reshape(4 * sec_b, bra_w, bra_w)

    code = (entries[..., 0] * 16 + entries[..., 1] * 4 + entries[..., 2]).astype(jnp.float32)
    mine = chans * EPW
    info = jnp.pad(jnp.stack([code.reshape(-1), coeffs.reshape(-1)]), ((0, 6), (0, 128 - mine)))

    env_all, bra_all, info_all = gather(
        env_in.reshape(chans * sec_b, bra_w, ket_w), bra, info, n, chans, sec_a, sec_b)
    bra_all = bra_all.reshape(4 * 4 * sec_b, bra_w, bra_w)

    code = info_all[:, 0, :mine].reshape(-1).astype(jnp.int32)
    value = info_all[:, 1, :mine].reshape(-1)
    wide = code.shape[0]
    code, value = jnp.tile(code, 2), jnp.tile(value, 2)
    index = jnp.arange(2 * wide, dtype=jnp.int32)
    q_b = index // wide
    w_in = (index % wide) // EPW
    w_out, sp, s = code // 16, (code // 4) % 4, code % 4
    up_a, up_b = s % 2, s // 2
    in_a, in_b = channel_charge(w_in)
    out_a, out_b = channel_charge(w_out)
    i = w_out - row * chans
    to_a, to_b = a + up_a + out_a, q_b + up_b + out_b

    def inside(x, count):
        return (x >= 0) & (x < count)

    live = (inside(i, chans) & inside(q_b + up_b, sec_b) & inside(a + up_a, sec_a)
            & inside(q_b + in_b, sec_b) & inside(a + in_a, sec_a)
            & inside(to_a, sec_a) & inside(to_b, sec_b))
    buckets = 2 * chans * 3
    key = jnp.where(live, (up_a * chans + i) * 3 + jnp.where(up_b == 0, q_b, 2), buckets)
    pack = (w_in * 2 + q_b) * 32 + (up_a + out_a + 1) * 8 + sp * 2 + to_b
    starts = jnp.sum(key[None, :] < jnp.arange(buckets + 1, dtype=jnp.int32)[:, None], axis=1, dtype=jnp.int32)
    order = key * (2 * wide) + index
    rank = jnp.sum(order[None, :] < order[:, None], axis=1, dtype=jnp.int32)
    hit = rank[None, :] == index[:, None]
    packed = jnp.sum(jnp.where(hit, pack[None, :], 0), axis=1, dtype=jnp.int32)
    values = jnp.sum(jnp.where(hit, value[None, :], 0.0), axis=1)

    ket = ket_mps.reshape(4 * sec_b, ket_w, ket_w)
    here = sizes_at(ket_ext, 1, 0, 0)
    above = sizes_at(ket_ext, 1, 1, 0)
    up = terms(1, chans, starts, packed, values, jnp.concatenate([here, above]), env_all, bra_all, ket, jnp.bfloat16)
    up = lax.ppermute(up, "sec", [(k, k + 1) for k in range(sec_a - 1)])
    same = terms(0, chans, starts, packed, values, jnp.concatenate([here, here]), env_all, bra_all, ket, jnp.float32)
    out = (same + up.astype(jnp.float32)).astype(env_in.dtype)
    return out.reshape(env_in.shape)


def solution(mesh):
    placed = (
        P("row", "sec", None, None, None),
        P(None, "sec", None, None, None),
        P(None, "sec", None, None, None),
        P(),
        P(),
        P("row", None, None),
        P("row", None),
    )
    return jax.shard_map(
        body,
        mesh=mesh,
        in_specs=placed,
        out_specs=P("row", "sec", None, None, None),
        check_vma=False,
    )
```

time: 1000 us -> 171 us (0.17)
  loops' own time: 339 us -> 0 us
  waiting for transfers between devices: 319 us -> 20 us
  local copies, waits for them, and re-layouts: 143 us -> 8.85 us
  matrix products: 133 us -> 0 us
  Pallas kernels: 0 us -> 131 us
  other arithmetic: 31.2 us -> 6.94 us
  between operations: 13.5 us -> 0.08 us
    another operation x33 -> x0, loops' own time: 339 us -> none  [the longest x32 297 us: step(): return lax.cond(inside, add_term, lambda acc: acc, partial_value)]
    reduce_scatter x1 -> x0, waiting for transfers between devices: 281 us -> none  [body(): lax.psum_scatter(lax.fori_loop(0, chans * EPW, step, jnp.zeros((count, 1,...]
    dot_general x32 -> x0, matrix products: 133 us -> none  [entry_term(): jnp.einsum('abij,abil->abjl', bra_blk, half, preferred_element_type=jnp.f...]
    pallas_call x0 -> x3, Pallas kernels: none -> 131 us  [the longest x1 115 us: gather(): pl.pallas_call(functools.partial(gather_kernel, n, chans, sec_a, sec_b),...]
    dynamic_slice x96 -> x2, local copies, waits for them, and re-layouts: 124 us -> 1.24 us  [sizes_at(): lax.dynamic_slice(ext, (a + shift_a + pad, jnp.int32(shift_b + pad)), (1,...]
    ppermute x4 -> x1, waiting for transfers between devices: 38.1 us -> 20 us  [body(): up = lax.ppermute(up, 'sec', [(k, k + 1) for k in range(sec_a - 1)])]
    concatenate x3 -> x1, other arithmetic: 13.9 us -> 0.08 us  [body(): jnp.concatenate([here, above])]
    convert_element_type x1 -> x3, other arithmetic: 17.3 us -> 3.68 us  [the longest x1 2.18 us: body(): out = (same + up.astype(jnp.float32)).astype(env_in.dtype)]
  transfers between devices with their start and end apart: 5 -> 1, of which waited for: 5 -> 1; matrix products, arithmetic and copies ran while one was open for 1% -> 0% of each run, Pallas kernels for 0% -> 5%
where the time goes in v1:
time: 171 us; the launch traced here: 169 us
  Pallas kernels  131 us (77%)
  waiting for transfers between devices  20 us (12%)
  local copies, waits for them, and re-layouts  8.85 us (5%)
  other arithmetic  6.94 us (4%)
  starting transfers between devices  1.92 us (1%)
    pallas_call x1, Pallas kernels, gather(): pl.pallas_call(functools.partial(gather_kernel, n, chans, sec_a, sec_b),...  115 us
    ppermute x1, waiting for transfers between devices, body(): up = lax.ppermute(up, 'sec', [(k, k + 1) for k in range(sec_a - 1)])  20 us
    pallas_call x2, Pallas kernels, terms(): pl.pallas_call(functools.partial(terms_kernel, up_a, chans), out_shape=ja...  16.1 us
    unnamed x12, local copies, waits for them, and re-layouts  4.41 us
  transfers between devices with their start and end apart: 1, of which 1 were waited for; matrix products, arithmetic and copies ran while one was open for 0% of the time, Pallas kernels for 5%

profile of v1, /device:TPU:30, one launch (start us, length us, event | category | flops | bytes accessed | tf_op | source)
XLA Modules:
  0.0 169.2 jit_solution(2847028545201896691)
XLA Ops:
  0.0 0.8 stack_reshape.4
  0.8 0.7 add_convert_fusion.1
  1.5 0.1 convert_element_type.38
  1.6 1.0 pad_dynamic-slice_fusion.2
  2.7 0.1 copy.11
  2.9 1.6 fusion
  4.5 1.3 copy.12
  5.8 0.6 select_maximum_fusion.info
  6.4 115.3 %gather_row.1 = (bf16[64,256,512]{2,1,0:T(8,128)(2,1)}, bf16[4,8,256,256]{3,2,1,0:T(8,128)(2,1)}, f32[8,8,128]{2,1,0:T(8,128)}) custom-call(bf16[8,256,512]{2,1,0:T(8,128)(2,1)} %bitcast.24, bf16[8,256,256]{2,1,0:T(8,128)(2,1)} %bitcast.23, f32[8,128]{1,0:T(8,128)} %select_maximum_fusion.info), custom_call_target="tpu_custom_call" | custom-call | tf_op jit(solution)/shard_map/gather_row/pallas_call | solution.py:154
  121.7 0.8 slice_reduce_fusion
  122.5 0.8 convert_reduce_fusion.2
  123.3 0.1 convert_element_type.40
  123.5 0.2 convert_reduce_fusion
  123.8 0.2 select_reduce_fusion.values
  124.0 0.2 select_reduce_fusion.1.packed
  124.1 0.1 convert_reduce_fusion.1.starts
  124.3 0.2 fusion.25
  124.6 2.2 %copy-done = bf16[4,1,2,512,512]{4,3,2,1,0:T(8,128)(2,1)S(1)} copy-done((bf16[4,1,2,512,512]{4,3,2,1,0:T(8,128)(2,1)S(1)}, bf16[4,1,2,512,512]{4,3,2,1,0:T(8,128)(2,1)}, u32[]{:S(2)}) %copy-start) | copy-done | bytes 4194328
  126.8 2.2 %copy-done.2 = bf16[4,8,256,256]{3,2,1,0:T(8,128)(2,1)S(1)} copy-done((bf16[4,8,256,256]{3,2,1,0:T(8,128)(2,1)S(1)}, bf16[4,8,256,256]{3,2,1,0:T(8,128)(2,1)}, u32[]{:S(2)}) %copy-start.2) | copy-done | bytes 4194328
  129.0 7.2 %terms_up.1 = bf16[8,256,512]{2,1,0:T(8,128)(2,1)S(1)} custom-call(s32[25]{0:T(128)S(1)} %convert_reduce_fusion.1.starts, s32[512]{0:T(512)S(1)} %select_reduce_fusion.1.packed, f32[512]{0:T(512)S(1)} %select_reduce_fusion.values, s32[4]{0:T(128)S(1)} %get-tuple-element.23.ksz, bf16[64,256,512]{2,1,0:T(8,128)(2,1)} %get-tuple-element.9.env, ...), custom_call_target="tpu_custom_call" | custom-call | flops 5000000000 | bytes 16777216 | tf_op jit(solution)/shard_map/terms_up/pallas_call | solution.py:225
  136.1 1.9 %collective-permute-start = (bf16[8,256,512]{2,1,0:T(8,128)(2,1)S(1)}, bf16[8,256,512]{2,1,0:T(8,128)(2,1)S(1)}, u32[]{:S(2)}, u32[]{:S(2)}) collective-permute-start(bf16[8,256,512]{2,1,0:T(8,128)(2,1)S(1)} %terms_up.1), channel_id=1, source_target_pairs={{0,8},{8,16},{16,24},{1,9},{9,17},{17,25},{2,10},{10,18},{18,26},{... | collective-permute-start | bytes 6291464 | tf_op jit(solution)/shard_map/ppermute | solution.py:302
  138.1 8.9 %terms_same.1 = f32[8,256,512]{2,1,0:T(8,128)S(1)} custom-call(s32[25]{0:T(128)S(1)} %convert_reduce_fusion.1.starts, s32[512]{0:T(512)S(1)} %select_reduce_fusion.1.packed, f32[512]{0:T(512)S(1)} %select_reduce_fusion.values, s32[4]{0:T(128)S(1)} %get-tuple-element.24.ksz, bf16[64,256,512]{2,1,0:T(8,128)(2,1)} %get-tuple-element.9.env, ...), custom_call_target="tpu_custom_call" | custom-call | flops 5000000000 | bytes 16777216 | tf_op jit(solution)/shard_map/terms_same/pallas_call | solution.py:225
  147.0 20.0 %collective-permute-done = bf16[8,256,512]{2,1,0:T(8,128)(2,1)S(1)} collective-permute-done((bf16[8,256,512]{2,1,0:T(8,128)(2,1)S(1)}, bf16[8,256,512]{2,1,0:T(8,128)(2,1)S(1)}, u32[]{:S(2)}, u32[]{:S(2)}) %collective-permute-start) | collective-permute-done | bytes 2097184 | tf_op jit(solution)/shard_map/ppermute | solution.py:302
  167.0 2.2 %add_convert_fusion = bf16[8,256,512]{2,1,0:T(8,128)(2,1)} fusion(f32[8,256,512]{2,1,0:T(8,128)S(1)} %terms_same.1, bf16[8,256,512]{2,1,0:T(8,128)(2,1)S(1)} %collective-permute-done), kind=kLoop, calls=%fused_computation | loop fusion | flops 3145728 | bytes 8388608 | tf_op jit(solution)/shard_map/convert_element_type | solution.py:304
  (16 shorter events, 0.4 us)
Async XLA Ops:
  0.0 124.3 %copy-start.3 = (s32[4,2]{0,1:T(2,128)S(1)}, s32[4,2]{0,1:T(2,128)}, u32[]{:S(2)}) copy-start(s32[4,2]{0,1:T(2,128)} %param.10) | copy-start | bytes 100
  124.6 2.2 %copy-start = (bf16[4,1,2,512,512]{4,3,2,1,0:T(8,128)(2,1)S(1)}, bf16[4,1,2,512,512]{4,3,2,1,0:T(8,128)(2,1)}, u32[]{:S(2)}) copy-start(bf16[4,1,2,512,512]{4,3,2,1,0:T(8,128)(2,1)} %param.8) | copy-start | bytes 12582916
  126.8 2.2 %copy-start.2 = (bf16[4,8,256,256]{3,2,1,0:T(8,128)(2,1)S(1)}, bf16[4,8,256,256]{3,2,1,0:T(8,128)(2,1)}, u32[]{:S(2)}) copy-start(bf16[4,8,256,256]{3,2,1,0:T(8,128)(2,1)} %get-tuple-element.10) | copy-start | bytes 12582916
  129.0 9.1 %copy-start.1 = (bf16[4,1,2,512,512]{4,3,2,1,0:T(8,128)(2,1)S(1)}, bf16[4,1,2,512,512]{4,3,2,1,0:T(8,128)(2,1)}, u32[]{:S(2)}) copy-start(bf16[4,1,2,512,512]{4,3,2,1,0:T(8,128)(2,1)} %param.8) | copy-start | bytes 12582916
  136.1 30.8 %collective-permute-start = (bf16[8,256,512]{2,1,0:T(8,128)(2,1)S(1)}, bf16[8,256,512]{2,1,0:T(8,128)(2,1)S(1)}, u32[]{:S(2)}, u32[]{:S(2)}) collective-permute-start(bf16[8,256,512]{2,1,0:T(8,128)(2,1)S(1)} %terms_up.1), channel_id=1, source_target_pairs={{0,8},{8,16},{16,24},{1,9},{9,17},{17,25},{2,10},{10,18},{18,26},{... | collective-permute-start | bytes 6291464 | tf_op jit(solution)/shard_map/ppermute | solution.py:302

commit v2 on v1

--- a/solution.py
+++ b/solution.py
@@ -31,6 +31,52 @@
     x = jnp.where(lax.rem(z, 2) == 0, 1 + t, wide - 1 - t)
     back = Z - 1 - (pos - Z * (wide - 1))
     return jnp.where(pos < Z * (wide - 1), z * wide + x, back * wide)
+
+
+@functools.lru_cache(maxsize=None)
+def hop_masks(n, chans, sec_b):
+    wide, half, blocks = n // Z, n // 2, chans * sec_b
+    order = [z * wide + (1 + t if z % 2 == 0 else wide - 1 - t) for z in range(Z) for t in range(wide - 1)]
+    order += [z * wide for z in reversed(range(Z))]
+    classes = []
+    for dead in (-1, None, 1):
+        items = []
+        for p, source in enumerate(order):
+            for b in range(blocks):
+                klass = (source * chans + b // sec_b) % 9
+                to_b = klass // 3 - 1 + b % sec_b
+                if 0 <= to_b < sec_b and klass % 3 - 1 != dead:
+                    items.append((p, source, b))
+        reach = {item: half - (item[2] * 2 >= blocks) for item in items}
+
+        def links(item, d):
+            p = item[0]
+            return [(0, (p + t) % n) for t in range(d)] + [(1, (p - 1 - t) % n) for t in range(n - 1 - d)]
+
+        load = {(way, j): 0 for way in (0, 1) for j in range(n)}
+        for item in items:
+            for link in links(item, reach[item]):
+                load[link] += 1
+        for _ in range(12):
+            for item in items:
+                for link in links(item, reach[item]):
+                    load[link] -= 1
+                costs = []
+                for d in range(half - 3, half + 3):
+                    extra = sum((load[link] + 1) ** 6 - load[link] ** 6 for link in links(item, d))
+                    costs.append((extra, abs(2 * d - n + 1), d))
+                reach[item] = min(costs)[2]
+                for link in links(item, reach[item]):
+                    load[link] += 1
+        classes.append((reach, max(load.values())))
+    hops = max(max(d, n - 1 - d) for reach, _ in classes for d in reach.values())
+    masks = [[[[0, 0, 0] for _ in range(blocks)] for _ in (0, 1)] for _ in range(hops)]
+    for c, (reach, _) in enumerate(classes):
+        for (p, source, b), d in reach.items():
+            for way, count in ((0, d), (1, n - 1 - d)):
+                for k in range(count):
+                    masks[k][way][b][c] |= 1 << source
+    return hops, masks, [top for _, top in classes]
 
 
 def gather_kernel(n, chans, sec_a, sec_b, env, bra, info, env_all, bra_all, info_all,
@@ -52,10 +98,15 @@
     count = 2 + jnp.minimum(a, 2) + jnp.minimum(sec_a - 1 - a, 2)
     pl.semaphore_wait(barrier, count)
 
-    def live(source, b):
-        c_a, c_b = channel_charge(source * chans + b // sec_b)
-        x, y = a + c_a, b % sec_b + c_b
-        return (x >= 0) & (x < sec_a) & (y >= 0) & (y < sec_b)
+    hops, masks, _ = hop_masks(n, chans, sec_b)
+
+    def used(k, way, b):
+        return k <= hops and any(masks[k - 1][way][b])
+
+    def carried(k, way, b, source):
+        low, inner, high = masks[k - 1][way][b]
+        mask = jnp.where(a == 0, low, jnp.where(a == sec_a - 1, high, inner))
+        return lax.rem(lax.shift_right_logical(mask, source), 2) == 1
 
     def source_at(k, way):
         return ring_row(lax.rem(pos + (n - k if way == 0 else k), n), n)
@@ -73,9 +124,6 @@
             src_ref=src, dst_ref=info_all.at[source],
             send_sem=isend.at[k - 1, way], recv_sem=irecv.at[k - 1, way],
             device_id={"row": left if way else right}, device_id_type=MESH)
-
-    def used(k, way, b):
-        return k < half or (b < blocks // 2) == (way == 0)
 
     def info_used(k, way):
         return k < half or way == 0
@@ -92,10 +140,10 @@
     for way in (0, 1):
         info_copy(1, way, row).start()
     for b in range(blocks):
-        @pl.when(live(row, b))
-        def _(b=b):
-            for way in (0, 1):
-                if used(1, way, b):
+        for way in (0, 1):
+            if used(1, way, b):
+                @pl.when(carried(1, way, b, row))
+                def _(b=b, way=way):
                     block_copy(1, way, b, row).start()
     for d, copy in bra_copies():
         @pl.when((a + d >= 0) & (a + d < sec_a))
@@ -109,30 +157,32 @@
     for copy in own:
         copy.start()
 
-    for k in range(1, half + 1):
+    for k in range(1, hops + 1):
         sources = [source_at(k, way) for way in (0, 1)]
         for way in (0, 1):
-            if info_used(k, way):
+            if k <= half and info_used(k, way):
                 info_copy(k, way, sources[way]).wait_recv()
                 if k < half and info_used(k + 1, way):
                     info_copy(k + 1, way, sources[way]).start()
         for b in range(blocks):
             for way in (0, 1):
                 if used(k, way, b):
-                    @pl.when(live(sources[way], b))
+                    @pl.when(carried(k, way, b, sources[way]))
                     def _(k=k, way=way, b=b):
                         block_copy(k, way, b, sources[way]).wait_recv()
-                        if k < half and used(k + 1, way, b):
-                            block_copy(k + 1, way, b, sources[way]).start()
-
-    for k in range(1, half + 1):
+                        if used(k + 1, way, b):
+                            @pl.when(carried(k + 1, way, b, sources[way]))
+                            def _():
+                                block_copy(k + 1, way, b, sources[way]).start()
+
+    for k in range(1, hops + 1):
         for way in (0, 1):
             source = row if k == 1 else source_at(k - 1, way)
-            if info_used(k, way):
+            if k <= half and info_used(k, way):
                 info_copy(k, way, source).wait_send()
             for b in range(blocks):
                 if used(k, way, b):
-                    @pl.when(live(source, b))
+                    @pl.when(carried(k, way, b, source))
                     def _(k=k, way=way, b=b, source=source):
                         block_copy(k, way, b, source).wait_send()
     for d, copy in bra_copies():
@@ -149,6 +199,7 @@
 
 def gather(env, bra, info, n, chans, sec_a, sec_b):
     half, blocks = n // 2, chans * sec_b
+    hops = hop_masks(n, chans, sec_b)[0]
     anywhere = pl.BlockSpec(memory_space=pl.ANY)
     dma = pltpu.SemaphoreType.DMA
     return pl.pallas_call(
@@ -161,7 +212,7 @@
         in_specs=[anywhere] * 3,
         out_specs=(anywhere,) * 3,
         scratch_shapes=[
-            dma((half, 2, blocks)), dma((half, 2, blocks)), dma((half, 2)), dma((half, 2)),
+            dma((hops, 2, blocks)), dma((hops, 2, blocks)), dma((half, 2)), dma((half, 2)),
             dma((3,)), dma((3,)), dma((3,)),
         ],
         compiler_params=pltpu.CompilerParams(collective_id=0, has_side_effects=True),
@@ -169,9 +220,16 @@
     )(env, bra, info)
 
 
-def terms_kernel(up_a, chans, starts, packed, values, ksz, env, bra, ket, out, buf, t_acc, acc, sems):
-    first = starts[up_a * chans * 3]
-    last = starts[(up_a + 1) * chans * 3]
+def terms_kernel(up_a, base, count, starts, packed, values, ksz, env, bra_hbm, ket_hbm, out,
+                 buf, bra, ket, t_acc, acc, sems, load):
+    first = starts[base * 3]
+    last = starts[(base + count) * 3]
+    loads = [pltpu.make_async_copy(bra_hbm.at[pl.ds(8 * up_a, 24)], bra, load.at[0])]
+    loads += [
+        pltpu.make_async_copy(ket_hbm.at[(up_a + 2 * (j // 2)) * 2 + j % 2], ket.at[j], load.at[1 + j])
+        for j in range(3)
+    ]
+    loads[0].start()
 
     def fetch(j):
         slot = lax.rem(j, DEPTH)
@@ -182,12 +240,17 @@
         def _(d=d):
             fetch(first + d).start()
 
+    for copy in loads[1:]:
+        copy.start()
     acc[...] = jnp.zeros_like(acc)
     cols = lax.broadcasted_iota(jnp.int32, t_acc.shape, 1)
 
+    for copy in loads:
+        copy.wait()
+
     def channel(i, carry):
         for kind, (up_b, q_b) in enumerate(((0, 0), (0, 1), (1, 0))):
-            bucket = (up_a * chans + i) * 3 + kind
+            bucket = (base + i) * 3 + kind
             begin, end = starts[bucket], starts[bucket + 1]
 
             @pl.when(end > begin)
@@ -196,7 +259,7 @@
 
                 def item(j, c):
                     fetch(j).wait()
-                    b = bra[lax.rem(packed[j], 32)]
+                    b = bra[lax.rem(packed[j], 32) - 8 * up_a]
                     e = buf[lax.rem(j, DEPTH)]
                     t_acc[...] += values[j] * jnp.dot(b, e, preferred_element_type=jnp.float32)
 
@@ -207,31 +270,33 @@
 
                 lax.fori_loop(begin, end, item, 0)
                 t = jnp.where(cols < ksz[q_b], t_acc[...], 0.0).astype(jnp.bfloat16)
-                k = ket[(up_a + 2 * up_b) * 2 + q_b]
+                k = ket[2 * up_b + q_b]
                 acc[i * 2 + up_b + q_b] += jnp.dot(t, k, preferred_element_type=jnp.float32)
         for p_b in (0, 1):
             block = acc[i * 2 + p_b]
             out[i * 2 + p_b] = jnp.where(cols < ksz[2 + p_b], block, 0.0).astype(out.dtype)
         return carry
 
-    lax.fori_loop(0, chans, channel, 0)
-
-
-def terms(up_a, chans, starts, packed, values, ksz, env, bra, ket, dtype):
+    lax.fori_loop(0, count, channel, 0)
+
+
+def terms(up_a, chans, at, count, starts, packed, values, ksz, env, bra, ket, dtype):
     rows, cols = env.shape[1:]
-    blocks = chans * 2
+    blocks = count * 2
     smem = pl.BlockSpec(memory_space=pltpu.SMEM)
-    vmem = pl.BlockSpec(memory_space=pltpu.VMEM)
     return pl.pallas_call(
-        functools.partial(terms_kernel, up_a, chans),
+        functools.partial(terms_kernel, up_a, up_a * chans + at, count),
         out_shape=jax.ShapeDtypeStruct((blocks, rows, cols), dtype),
-        in_specs=[smem] * 4 + [pl.BlockSpec(memory_space=pl.ANY), vmem, vmem],
-        out_specs=vmem,
+        in_specs=[smem] * 4 + [pl.BlockSpec(memory_space=pl.ANY)] * 3,
+        out_specs=pl.BlockSpec(memory_space=pltpu.VMEM),
         scratch_shapes=[
             pltpu.VMEM((DEPTH, rows, cols), env.dtype),
+            pltpu.VMEM((24,) + bra.shape[1:], bra.dtype),
+            pltpu.VMEM((3,) + ket.shape[1:], ket.dtype),
             pltpu.VMEM((rows, cols), jnp.float32),
             pltpu.VMEM((blocks, rows, cols), jnp.float32),
             pltpu.SemaphoreType.DMA((DEPTH,)),
+            pltpu.SemaphoreType.DMA((4,)),
         ],
         compiler_params=pltpu.CompilerParams(vmem_limit_bytes=40 * 1024 * 1024),
         cost_estimate=pl.CostEstimate(flops=5 * 10**9, bytes_accessed=16 * 2**20, transcendentals=0),
@@ -298,10 +363,15 @@
     ket = ket_mps.reshape(4 * sec_b, ket_w, ket_w)
     here = sizes_at(ket_ext, 1, 0, 0)
     above = sizes_at(ket_ext, 1, 1, 0)
-    up = terms(1, chans, starts, packed, values, jnp.concatenate([here, above]), env_all, bra_all, ket, jnp.bfloat16)
-    up = lax.ppermute(up, "sec", [(k, k + 1) for k in range(sec_a - 1)])
-    same = terms(0, chans, starts, packed, values, jnp.concatenate([here, here]), env_all, bra_all, ket, jnp.float32)
-    out = (same + up.astype(jnp.float32)).astype(env_in.dtype)
+    sent = []
+    part = chans // 2
+    for at in (0, part):
+        up = terms(1, chans, at, part, starts, packed, values, jnp.concatenate([here, above]),
+                   env_all, bra_all, ket, jnp.bfloat16)
+        sent.append(lax.ppermute(up, "sec", [(k, k + 1) for k in range(sec_a - 1)]))
+    same = terms(0, chans, 0, chans, starts, packed, values, jnp.concatenate([here, here]),
+                 env_all, bra_all, ket, jnp.float32)
+    out = (same + jnp.concatenate(sent).astype(jnp.float32)).astype(env_in.dtype)
     return out.reshape(env_in.shape)
 
 

time: 171 us -> 168 us (0.982)
  waiting for transfers between devices: 20 us -> 7.18 us
  Pallas kernels: 131 us -> 139 us
  starting transfers between devices: 1.92 us -> 4.1 us
    ppermute x1 -> x2, waiting for transfers between devices: 20 us -> 7.18 us  [body(): sent.append(lax.ppermute(up, 'sec', [(k, k + 1) for k in range(sec_a - 1)]))]
    pallas_call x2 -> x3, Pallas kernels: 16.1 us -> 20.1 us  [terms(): pl.pallas_call(functools.partial(terms_kernel, up_a, up_a * chans + at, c...]
    pallas_call x1, Pallas kernels: 115 us -> 119 us  [gather(): pl.pallas_call(functools.partial(gather_kernel, n, chans, sec_a, sec_b),...]
    ppermute x1 -> x2, starting transfers between devices: 1.92 us -> 4.1 us  [body(): sent.append(lax.ppermute(up, 'sec', [(k, k + 1) for k in range(sec_a - 1)]))]
  transfers between devices with their start and end apart: 1 -> 2, of which waited for: 1 -> 1; matrix products, arithmetic and copies ran while one was open for 0% -> 0% of each run, Pallas kernels for 5% -> 10%
where the time goes in v2:
time: 168 us; the launch traced here: 166 us
  Pallas kernels  139 us (83%)
  local copies, waits for them, and re-layouts  8.85 us (5%)
  waiting for transfers between devices  7.18 us (4%)
  other arithmetic  6.8 us (4%)
  starting transfers between devices  4.1 us (2%)
    pallas_call x1, Pallas kernels, gather(): pl.pallas_call(functools.partial(gather_kernel, n, chans, sec_a, sec_b),...  119 us
    pallas_call x3, Pallas kernels, terms(): pl.pallas_call(functools.partial(terms_kernel, up_a, up_a * chans + at, c...  20.1 us
    ppermute x2, waiting for transfers between devices, body(): sent.append(lax.ppermute(up, 'sec', [(k, k + 1) for k in range(sec_a - 1)]))  7.18 us
    unnamed x12, local copies, waits for them, and re-layouts  4.41 us
    ppermute x2, starting transfers between devices, body(): sent.append(lax.ppermute(up, 'sec', [(k, k + 1) for k in range(sec_a - 1)]))  4.1 us
  transfers between devices with their start and end apart: 2, of which 1 were waited for; matrix products, arithmetic and copies ran while one was open for 0% of the time, Pallas kernels for 10%

profile of v2, /device:TPU:30, one launch (start us, length us, event | category | flops | bytes accessed | tf_op | source)
XLA Modules:
  0.0 165.9 jit_solution(9136299314519785555)
XLA Ops:
  0.0 0.8 stack_reshape.4
  0.8 0.7 add_convert_fusion.1
  1.6 1.0 pad_dynamic-slice_fusion.2
  2.7 0.1 copy.11
  2.9 1.6 fusion
  4.5 1.3 copy.12
  5.8 0.6 select_maximum_fusion.info
  6.4 118.8 %gather_row.1 = (bf16[64,256,512]{2,1,0:T(8,128)(2,1)}, bf16[4,8,256,256]{3,2,1,0:T(8,128)(2,1)}, f32[8,8,128]{2,1,0:T(8,128)}) custom-call(bf16[8,256,512]{2,1,0:T(8,128)(2,1)} %bitcast.26, bf16[8,256,256]{2,1,0:T(8,128)(2,1)} %bitcast.25, f32[8,128]{1,0:T(8,128)} %select_maximum_fusion.info), custom_call_target="tpu_custom_call" | custom-call | tf_op jit(solution)/shard_map/gather_row/pallas_call | solution.py:205
  125.2 0.8 slice_reduce_fusion
  126.0 0.8 convert_reduce_fusion.2
  127.0 0.2 convert_reduce_fusion
  127.2 0.2 select_reduce_fusion.values
  127.4 0.2 select_reduce_fusion.1.packed
  127.6 0.1 convert_reduce_fusion.1.starts
  127.7 0.2 fusion.25
  128.0 2.2 %copy-done = bf16[4,1,2,512,512]{4,3,2,1,0:T(8,128)(2,1)S(1)} copy-done((bf16[4,1,2,512,512]{4,3,2,1,0:T(8,128)(2,1)S(1)}, bf16[4,1,2,512,512]{4,3,2,1,0:T(8,128)(2,1)}, u32[]{:S(2)}) %copy-start) | copy-done | bytes 4194328
  130.2 2.2 %copy-done.2 = bf16[4,8,256,256]{3,2,1,0:T(8,128)(2,1)S(1)} copy-done((bf16[4,8,256,256]{3,2,1,0:T(8,128)(2,1)S(1)}, bf16[4,8,256,256]{3,2,1,0:T(8,128)(2,1)}, u32[]{:S(2)}) %copy-start.2) | copy-done | bytes 4194328
  132.4 3.8 %terms_up.2 = bf16[4,256,512]{2,1,0:T(8,128)(2,1)S(1)} custom-call(s32[25]{0:T(128)S(1)} %convert_reduce_fusion.1.starts, s32[512]{0:T(512)S(1)} %select_reduce_fusion.1.packed, f32[512]{0:T(512)S(1)} %select_reduce_fusion.values, s32[4]{0:T(128)S(1)} %get-tuple-element.23.ksz, bf16[64,256,512]{2,1,0:T(8,128)(2,1)} %get-tuple-element.9.env, ...), custom_call_target="tpu_custom_call" | custom-call | flops 5000000000 | bytes 16777216 | tf_op jit(solution)/shard_map/terms_up/pallas_call | solution.py:287
  136.2 2.2 %collective-permute-start = (bf16[4,256,512]{2,1,0:T(8,128)(2,1)S(1)}, bf16[4,256,512]{2,1,0:T(8,128)(2,1)S(1)}, u32[]{:S(2)}, u32[]{:S(2)}) collective-permute-start(bf16[4,256,512]{2,1,0:T(8,128)(2,1)S(1)} %terms_up.2), channel_id=1, source_target_pairs={{0,8},{8,16},{16,24},{1,9},{9,17},{17,25},{2,10},{10,18},{18,26},{... | collective-permute-start | bytes 3145736 | tf_op jit(solution)/shard_map/ppermute | solution.py:371
  138.4 6.7 %terms_up.3 = bf16[4,256,512]{2,1,0:T(8,128)(2,1)S(1)} custom-call(s32[25]{0:T(128)S(1)} %convert_reduce_fusion.1.starts, s32[512]{0:T(512)S(1)} %select_reduce_fusion.1.packed, f32[512]{0:T(512)S(1)} %select_reduce_fusion.values, s32[4]{0:T(128)S(1)} %get-tuple-element.23.ksz, bf16[64,256,512]{2,1,0:T(8,128)(2,1)} %get-tuple-element.9.env, ...), custom_call_target="tpu_custom_call" | custom-call | flops 5000000000 | bytes 16777216 | tf_op jit(solution)/shard_map/terms_up/pallas_call | solution.py:287
  145.1 1.9 %collective-permute-start.1 = (bf16[4,256,512]{2,1,0:T(8,128)(2,1)S(1)}, bf16[4,256,512]{2,1,0:T(8,128)(2,1)S(1)}, u32[]{:S(2)}, u32[]{:S(2)}) collective-permute-start(bf16[4,256,512]{2,1,0:T(8,128)(2,1)S(1)} %terms_up.3), channel_id=1, source_target_pairs={{0,8},{8,16},{16,24},{1,9},{9,17},{17,25},{2,10},{10,18},{18,26},{... | collective-permute-start | bytes 3145736 | tf_op jit(solution)/shard_map/ppermute | solution.py:371
  147.1 9.6 %terms_same.1 = f32[8,256,512]{2,1,0:T(8,128)S(1)} custom-call(s32[25]{0:T(128)S(1)} %convert_reduce_fusion.1.starts, s32[512]{0:T(512)S(1)} %select_reduce_fusion.1.packed, f32[512]{0:T(512)S(1)} %select_reduce_fusion.values, s32[4]{0:T(128)S(1)} %get-tuple-element.24.ksz, bf16[64,256,512]{2,1,0:T(8,128)(2,1)} %get-tuple-element.9.env, ...), custom_call_target="tpu_custom_call" | custom-call | flops 5000000000 | bytes 16777216 | tf_op jit(solution)/shard_map/terms_same/pallas_call | solution.py:287
  156.7 7.2 %collective-permute-done.1 = bf16[4,256,512]{2,1,0:T(8,128)(2,1)S(1)} collective-permute-done((bf16[4,256,512]{2,1,0:T(8,128)(2,1)S(1)}, bf16[4,256,512]{2,1,0:T(8,128)(2,1)S(1)}, u32[]{:S(2)}, u32[]{:S(2)}) %collective-permute-start.1) | collective-permute-done | bytes 1048608 | tf_op jit(solution)/shard_map/ppermute | solution.py:371
  163.9 2.0 %add_convert_fusion = bf16[8,256,512]{2,1,0:T(8,128)(2,1)} fusion(f32[8,256,512]{2,1,0:T(8,128)S(1)} %terms_same.1, bf16[4,256,512]{2,1,0:T(8,128)(2,1)S(1)} %collective-permute-done.1, bf16[4,256,512]{2,1,0:T(8,128)(2,1)S(1)} %collective-permute-done), kind=kLoop, calls=%fused_computation | loop fusion | flops 4194304 | bytes 8388608 | tf_op jit(solution)/shard_map/convert_element_type | solution.py:374
  (19 shorter events, 0.6 us)
Async XLA Ops:
  0.0 127.7 %copy-start.3 = (s32[4,2]{0,1:T(2,128)S(1)}, s32[4,2]{0,1:T(2,128)}, u32[]{:S(2)}) copy-start(s32[4,2]{0,1:T(2,128)} %param.10) | copy-start | bytes 100
  128.0 2.2 %copy-start = (bf16[4,1,2,512,512]{4,3,2,1,0:T(8,128)(2,1)S(1)}, bf16[4,1,2,512,512]{4,3,2,1,0:T(8,128)(2,1)}, u32[]{:S(2)}) copy-start(bf16[4,1,2,512,512]{4,3,2,1,0:T(8,128)(2,1)} %param.8) | copy-start | bytes 12582916
  130.2 2.2 %copy-start.2 = (bf16[4,8,256,256]{3,2,1,0:T(8,128)(2,1)S(1)}, bf16[4,8,256,256]{3,2,1,0:T(8,128)(2,1)}, u32[]{:S(2)}) copy-start(bf16[4,8,256,256]{3,2,1,0:T(8,128)(2,1)} %get-tuple-element.10) | copy-start | bytes 12582916
  136.2 10.8 %copy-start.1 = (bf16[4,1,2,512,512]{4,3,2,1,0:T(8,128)(2,1)S(1)}, bf16[4,1,2,512,512]{4,3,2,1,0:T(8,128)(2,1)}, u32[]{:S(2)}) copy-start(bf16[4,1,2,512,512]{4,3,2,1,0:T(8,128)(2,1)} %param.8) | copy-start | bytes 12582916
  136.2 20.4 %collective-permute-start = (bf16[4,256,512]{2,1,0:T(8,128)(2,1)S(1)}, bf16[4,256,512]{2,1,0:T(8,128)(2,1)S(1)}, u32[]{:S(2)}, u32[]{:S(2)}) collective-permute-start(bf16[4,256,512]{2,1,0:T(8,128)(2,1)S(1)} %terms_up.2), channel_id=1, source_target_pairs={{0,8},{8,16},{16,24},{1,9},{9,17},{17,25},{2,10},{10,18},{18,26},{... | collective-permute-start | bytes 3145736 | tf_op jit(solution)/shard_map/ppermute | solution.py:371
  145.1 18.7 %collective-permute-start.1 = (bf16[4,256,512]{2,1,0:T(8,128)(2,1)S(1)}, bf16[4,256,512]{2,1,0:T(8,128)(2,1)S(1)}, u32[]{:S(2)}, u32[]{:S(2)}) collective-permute-start(bf16[4,256,512]{2,1,0:T(8,128)(2,1)S(1)} %terms_up.3), channel_id=1, source_target_pairs={{0,8},{8,16},{16,24},{1,9},{9,17},{17,25},{2,10},{10,18},{18,26},{... | collective-permute-start | bytes 3145736 | tf_op jit(solution)/shard_map/ppermute | solution.py:371

commit v3 on v2

--- a/solution.py
+++ b/solution.py
@@ -79,8 +79,8 @@
     return hops, masks, [top for _, top in classes]
 
 
-def gather_kernel(n, chans, sec_a, sec_b, env, bra, info, env_all, bra_all, info_all,
-                  send, recv, isend, irecv, bsend, brecv, local):
+def gather_kernel(n, chans, sec_a, sec_b, sizes, env, bra_hbm, info, env_all, bra_all, info_all,
+                  env_own, bra_raw, bra, send, recv, isend, irecv, bsend, brecv, local):
     a = lax.axis_index("sec")
     row = lax.axis_index("row")
     pos = ring_pos(row, n)
@@ -145,16 +145,38 @@
                 @pl.when(carried(1, way, b, row))
                 def _(b=b, way=way):
                     block_copy(1, way, b, row).start()
+    loads = (
+        pltpu.make_async_copy(bra_hbm, bra_raw, local.at[0]),
+        pltpu.make_async_copy(env, env_own, local.at[1]),
+    )
+    for copy in loads:
+        copy.start()
+    info_own = pltpu.make_async_copy(info, info_all.at[row], local.at[2])
+    info_own.start()
+
+    def size_at(x, y):
+        inner = jnp.where((x >= 0) & (y >= 0), sizes[jnp.maximum(x, 0) * sec_b + max(y, 0)], 0)
+        return inner
+
+    loads[0].wait()
+    at_row = lax.broadcasted_iota(jnp.int32, bra.shape[1:], 0)
+    at_col = lax.broadcasted_iota(jnp.int32, bra.shape[1:], 1)
+    for j in range(4 * sec_b):
+        sp, y = j // sec_b, j % sec_b
+        keep = (at_row < size_at(a - sp % 2, y - sp // 2)) & (at_col < size_at(a, y))
+        block = jnp.where(keep, bra_raw[j].astype(jnp.float32), 0.0)
+        bra[j] = block.T.astype(bra.dtype)
     for d, copy in bra_copies():
         @pl.when((a + d >= 0) & (a + d < sec_a))
         def _(copy=copy):
             copy.start()
+    loads[1].wait()
     own = (
-        pltpu.make_async_copy(env, env_all.at[pl.ds(row * blocks, blocks)], local.at[0]),
-        pltpu.make_async_copy(bra, bra_all.at[1], local.at[1]),
-        pltpu.make_async_copy(info, info_all.at[row], local.at[2]),
+        pltpu.make_async_copy(env_own, env_all.at[pl.ds(row * blocks, blocks)], local.at[1]),
+        pltpu.make_async_copy(bra, bra_all.at[1], local.at[0]),
+        info_own,
     )
-    for copy in own:
+    for copy in own[:2]:
         copy.start()
 
     for k in range(1, hops + 1):
@@ -197,7 +219,7 @@
         copy.wait()
 
 
-def gather(env, bra, info, n, chans, sec_a, sec_b):
+def gather(sizes, env, bra, info, n, chans, sec_a, sec_b):
     half, blocks = n // 2, chans * sec_b
     hops = hop_masks(n, chans, sec_b)[0]
     anywhere = pl.BlockSpec(memory_space=pl.ANY)
@@ -209,15 +231,17 @@
             jax.ShapeDtypeStruct((4,) + bra.shape, bra.dtype),
             jax.ShapeDtypeStruct((n,) + info.shape, info.dtype),
         ),
-        in_specs=[anywhere] * 3,
+        in_specs=[pl.BlockSpec(memory_space=pltpu.SMEM)] + [anywhere] * 3,
         out_specs=(anywhere,) * 3,
         scratch_shapes=[
+            pltpu.VMEM(env.shape, env.dtype), pltpu.VMEM(bra.shape, bra.dtype), pltpu.VMEM(bra.shape, bra.dtype),
             dma((hops, 2, blocks)), dma((hops, 2, blocks)), dma((half, 2)), dma((half, 2)),
             dma((3,)), dma((3,)), dma((3,)),
         ],
-        compiler_params=pltpu.CompilerParams(collective_id=0, has_side_effects=True),
+        compiler_params=pltpu.CompilerParams(
+            collective_id=0, has_side_effects=True, vmem_limit_bytes=60 * 1024 * 1024),
         name="gather_row",
-    )(env, bra, info)
+    )(sizes, env, bra, info)
 
 
 def terms_kernel(up_a, base, count, starts, packed, values, ksz, env, bra_hbm, ket_hbm, out,
@@ -298,7 +322,7 @@
             pltpu.SemaphoreType.DMA((DEPTH,)),
             pltpu.SemaphoreType.DMA((4,)),
         ],
-        compiler_params=pltpu.CompilerParams(vmem_limit_bytes=40 * 1024 * 1024),
+        compiler_params=pltpu.CompilerParams(vmem_limit_bytes=60 * 1024 * 1024),
         cost_estimate=pl.CostEstimate(flops=5 * 10**9, bytes_accessed=16 * 2**20, transcendentals=0),
         name="terms_up" if up_a else "terms_same",
     )(starts, packed, values, ksz, env, bra, ket)
@@ -310,24 +334,17 @@
     row = lax.axis_index("row")
     sec_a, n = lax.axis_size("sec"), lax.axis_size("row")
     ket_ext = jnp.pad(ket_sizes, 1)
-    bra_ext = jnp.pad(bra_sizes, 2)
 
     def sizes_at(ext, pad, shift_a, shift_b):
         return lax.dynamic_slice(ext, (a + shift_a + pad, jnp.int32(shift_b + pad)), (1, sec_b))[0]
 
-    own = sizes_at(bra_ext, 2, 0, 0)
-    src = jnp.stack([sizes_at(bra_ext, 2, -(sp % 2), -(sp // 2)) for sp in range(4)])
-    at = jnp.arange(bra_w, dtype=jnp.int32)
-    keep = (at[None, None, :, None] < src[:, :, None, None]) & (at < own[None, :, None, None])
-    bra = jnp.where(keep, bra_mps[:, 0], jnp.zeros((), bra_mps.dtype)).swapaxes(2, 3)
-    bra = bra.reshape(4 * sec_b, bra_w, bra_w)
-
+    bra = bra_mps.reshape(4 * sec_b, bra_w, bra_w)
     code = (entries[..., 0] * 16 + entries[..., 1] * 4 + entries[..., 2]).astype(jnp.float32)
     mine = chans * EPW
     info = jnp.pad(jnp.stack([code.reshape(-1), coeffs.reshape(-1)]), ((0, 6), (0, 128 - mine)))
 
     env_all, bra_all, info_all = gather(
-        env_in.reshape(chans * sec_b, bra_w, ket_w), bra, info, n, chans, sec_a, sec_b)
+        bra_sizes.reshape(-1), env_in.reshape(chans * sec_b, bra_w, ket_w), bra, info, n, chans, sec_a, sec_b)
     bra_all = bra_all.reshape(4 * 4 * sec_b, bra_w, bra_w)
 
     code = info_all[:, 0, :mine].reshape(-1).astype(jnp.int32)

time: 168 us -> 171 us (1.018)
  the two profiles are of different devices: /device:TPU:30 before, /device:TPU:22 now
where the time goes in v3:
time: 171 us
  Pallas kernels  149 us (87%)
  other arithmetic  9.55 us (6%)
  waiting for transfers between devices  4.65 us (3%)
  local copies, waits for them, and re-layouts  4.11 us (2%)
  starting transfers between devices  3.84 us (2%)
    pallas_call x1, Pallas kernels, gather(): pl.pallas_call(functools.partial(gather_kernel, n, chans, sec_a, sec_b),...  122 us
    pallas_call x3, Pallas kernels, terms(): pl.pallas_call(functools.partial(terms_kernel, up_a, up_a * chans + at, c...  26.8 us
    ppermute x2, waiting for transfers between devices, body(): sent.append(lax.ppermute(up, 'sec', [(k, k + 1) for k in range(sec_a - 1)]))  4.65 us
    convert_element_type x1, other arithmetic, body(): (same + jnp.concatenate(sent).astype(jnp.float32)).astype(env_in.dtype)  4.23 us
    ppermute x2, starting transfers between devices, body(): sent.append(lax.ppermute(up, 'sec', [(k, k + 1) for k in range(sec_a - 1)]))  3.84 us
  transfers between devices with their start and end apart: 2, of which 1 were waited for; matrix products, arithmetic and copies ran while one was open for 0% of the time, Pallas kernels for 11%

profile of v3, /device:TPU:22, one launch (start us, length us, event | category | flops | bytes accessed | tf_op | source)
XLA Modules:
  0.0 170.8 jit_solution(9870300998333485730)
XLA Ops:
  0.0 0.8 stack_reshape.4
  0.8 0.8 copy.12
  1.5 0.6 reshape.462.sizes
  2.1 0.7 add_convert_fusion.1
  2.8 0.1 convert_element_type.38
  2.9 0.6 select_maximum_fusion.info
  3.5 121.8 %gather_row.1 = (bf16[64,256,512]{2,1,0:T(8,128)(2,1)}, bf16[4,8,256,256]{3,2,1,0:T(8,128)(2,1)}, f32[8,8,128]{2,1,0:T(8,128)}) custom-call(s32[8]{0:T(128)} %reshape.462.sizes, bf16[8,256,512]{2,1,0:T(8,128)(2,1)} %bitcast.21, bf16[8,256,256]{2,1,0:T(8,128)(2,1)} %bitcast.22, f32[8,128]{1,0:T(8,128)} %select_maximum_fusion.info), custom_call_target="tpu_custom_call" | custom-call | tf_op jit(solution)/shard_map/gather_row/pallas_call | solution.py:227
  125.3 0.8 slice_reduce_fusion
  126.1 0.8 convert_reduce_fusion.2
  126.9 0.1 convert_element_type.40
  126.9 0.1 tile.18
  127.1 0.2 convert_reduce_fusion
  127.3 0.8 select_reduce_fusion.values
  128.1 0.8 select_reduce_fusion.1.packed
  128.9 0.7 convert_reduce_fusion.1.starts
  129.6 1.0 fusion.24
  130.6 0.7 pad_add_fusion.1
  131.2 7.8 %terms_up.2 = bf16[4,256,512]{2,1,0:T(8,128)(2,1)} custom-call(s32[25]{0:T(128)} %convert_reduce_fusion.1.starts, s32[512]{0:T(512)} %select_reduce_fusion.1.packed, f32[512]{0:T(512)} %select_reduce_fusion.values, s32[4]{0:T(128)} %get-tuple-element.16.ksz, bf16[64,256,512]{2,1,0:T(8,128)(2,1)} %get-tuple-element.9.env, bf16[32,256,256]{2,1,0:T(8,128)(2,1)} %bitcast.18, ...), custom_call_target="tpu_custom_call" | custom-call | flops 5000000000 | bytes 16777216 | tf_op jit(solution)/shard_map/terms_up/pallas_call | solution.py:311
  139.0 1.9 %collective-permute-start = (bf16[4,256,512]{2,1,0:T(8,128)(2,1)}, bf16[4,256,512]{2,1,0:T(8,128)(2,1)S(1)}, u32[]{:S(2)}, u32[]{:S(2)}) collective-permute-start(bf16[4,256,512]{2,1,0:T(8,128)(2,1)} %terms_up.2), channel_id=1, source_target_pairs={{0,8},{8,16},{16,24},{1,9},{9,17},{17,25},{2,10},{10,18},{18,26},{... | collective-permute-start | bytes 3145736 | tf_op jit(solution)/shard_map/ppermute | solution.py:388
  140.9 7.4 %terms_up.3 = bf16[4,256,512]{2,1,0:T(8,128)(2,1)} custom-call(s32[25]{0:T(128)} %convert_reduce_fusion.1.starts, s32[512]{0:T(512)} %select_reduce_fusion.1.packed, f32[512]{0:T(512)} %select_reduce_fusion.values, s32[4]{0:T(128)} %get-tuple-element.16.ksz, bf16[64,256,512]{2,1,0:T(8,128)(2,1)} %get-tuple-element.9.env, bf16[32,256,256]{2,1,0:T(8,128)(2,1)} %bitcast.19, ...), custom_call_target="tpu_custom_call" | custom-call | flops 5000000000 | bytes 16777216 | tf_op jit(solution)/shard_map/terms_up/pallas_call | solution.py:311
  148.4 1.9 %collective-permute-start.1 = (bf16[4,256,512]{2,1,0:T(8,128)(2,1)}, bf16[4,256,512]{2,1,0:T(8,128)(2,1)S(1)}, u32[]{:S(2)}, u32[]{:S(2)}) collective-permute-start(bf16[4,256,512]{2,1,0:T(8,128)(2,1)} %terms_up.3), channel_id=1, source_target_pairs={{0,8},{8,16},{16,24},{1,9},{9,17},{17,25},{2,10},{10,18},{18,26},{... | collective-permute-start | bytes 3145736 | tf_op jit(solution)/shard_map/ppermute | solution.py:388
  150.3 11.6 %terms_same.1 = f32[8,256,512]{2,1,0:T(8,128)} custom-call(s32[25]{0:T(128)} %convert_reduce_fusion.1.starts, s32[512]{0:T(512)} %select_reduce_fusion.1.packed, f32[512]{0:T(512)} %select_reduce_fusion.values, s32[4]{0:T(128)} %get-tuple-element.17.ksz, bf16[64,256,512]{2,1,0:T(8,128)(2,1)} %get-tuple-element.9.env, bf16[32,256,256]{2,1,0:T(8,128)(2,1)} %bitcast.20, ...), custom_call_target="tpu_custom_call" | custom-call | flops 5000000000 | bytes 16777216 | tf_op jit(solution)/shard_map/terms_same/pallas_call | solution.py:311
  161.9 4.6 %collective-permute-done.1 = bf16[4,256,512]{2,1,0:T(8,128)(2,1)S(1)} collective-permute-done((bf16[4,256,512]{2,1,0:T(8,128)(2,1)}, bf16[4,256,512]{2,1,0:T(8,128)(2,1)S(1)}, u32[]{:S(2)}, u32[]{:S(2)}) %collective-permute-start.1) | collective-permute-done | bytes 1048608 | tf_op jit(solution)/shard_map/ppermute | solution.py:388
  166.6 4.2 %add_convert_fusion = bf16[8,256,512]{2,1,0:T(8,128)(2,1)} fusion(f32[8,256,512]{2,1,0:T(8,128)} %terms_same.1, bf16[4,256,512]{2,1,0:T(8,128)(2,1)S(1)} %collective-permute-done.1, bf16[4,256,512]{2,1,0:T(8,128)(2,1)S(1)} %collective-permute-done), kind=kLoop, calls=%fused_computation | loop fusion | flops 4194304 | bytes 8388608 | tf_op jit(solution)/shard_map/convert_element_type | solution.py:391
  (6 shorter events, 0.1 us)
Async XLA Ops:
  139.0 22.9 %collective-permute-start = (bf16[4,256,512]{2,1,0:T(8,128)(2,1)}, bf16[4,256,512]{2,1,0:T(8,128)(2,1)S(1)}, u32[]{:S(2)}, u32[]{:S(2)}) collective-permute-start(bf16[4,256,512]{2,1,0:T(8,128)(2,1)} %terms_up.2), channel_id=1, source_target_pairs={{0,8},{8,16},{16,24},{1,9},{9,17},{17,25},{2,10},{10,18},{18,26},{... | collective-permute-start | bytes 3145736 | tf_op jit(solution)/shard_map/ppermute | solution.py:388
  148.4 18.2 %collective-permute-start.1 = (bf16[4,256,512]{2,1,0:T(8,128)(2,1)}, bf16[4,256,512]{2,1,0:T(8,128)(2,1)S(1)}, u32[]{:S(2)}, u32[]{:S(2)}) collective-permute-start(bf16[4,256,512]{2,1,0:T(8,128)(2,1)} %terms_up.3), channel_id=1, source_target_pairs={{0,8},{8,16},{16,24},{1,9},{9,17},{17,25},{2,10},{10,18},{18,26},{... | collective-permute-start | bytes 3145736 | tf_op jit(solution)/shard_map/ppermute | solution.py:388

commit v4 on v3

--- a/solution.py
+++ b/solution.py
@@ -38,8 +38,9 @@
     wide, half, blocks = n // Z, n // 2, chans * sec_b
     order = [z * wide + (1 + t if z % 2 == 0 else wide - 1 - t) for z in range(Z) for t in range(wide - 1)]
     order += [z * wide for z in reversed(range(Z))]
-    classes = []
-    for dead in (-1, None, 1):
+    classes = {}
+    shared = None
+    for dead in (None, -1, 1):
         items = []
         for p, source in enumerate(order):
             for b in range(blocks):
@@ -53,7 +54,7 @@
             p = item[0]
             return [(0, (p + t) % n) for t in range(d)] + [(1, (p - 1 - t) % n) for t in range(n - 1 - d)]
 
-        load = {(way, j): 0 for way in (0, 1) for j in range(n)}
+        load = dict(shared) if shared else {(way, j): 0 for way in (0, 1) for j in range(n)}
         for item in items:
             for link in links(item, reach[item]):
                 load[link] += 1
@@ -62,13 +63,15 @@
                 for link in links(item, reach[item]):
                     load[link] -= 1
                 costs = []
-                for d in range(half - 3, half + 3):
+                for d in range(half - 2, half + 2):
                     extra = sum((load[link] + 1) ** 6 - load[link] ** 6 for link in links(item, d))
                     costs.append((extra, abs(2 * d - n + 1), d))
                 reach[item] = min(costs)[2]
                 for link in links(item, reach[item]):
                     load[link] += 1
-        classes.append((reach, max(load.values())))
+        classes[dead] = (reach, max(load.values()))
+        shared = shared or load
+    classes = [classes[dead] for dead in (-1, None, 1)]
     hops = max(max(d, n - 1 - d) for reach, _ in classes for d in reach.values())
     masks = [[[[0, 0, 0] for _ in range(blocks)] for _ in (0, 1)] for _ in range(hops)]
     for c, (reach, _) in enumerate(classes):
@@ -79,8 +82,72 @@
     return hops, masks, [top for _, top in classes]
 
 
-def gather_kernel(n, chans, sec_a, sec_b, sizes, env, bra_hbm, info, env_all, bra_all, info_all,
-                  env_own, bra_raw, bra, send, recv, isend, irecv, bsend, brecv, local):
+def fill_lists(n, chans, sec_a, sec_b, a, row, info, info_all, held, ints, floats, sem):
+    for source in range(n):
+        @pl.when(row == source)
+        def _(source=source):
+            copy = pltpu.make_async_copy(info, held.at[source], sem)
+            copy.start()
+            copy.wait()
+
+        @pl.when(row != source)
+        def _(source=source):
+            copy = pltpu.make_async_copy(info_all.at[source], held.at[source], sem)
+            copy.start()
+            copy.wait()
+    mine = chans * EPW
+    wide = n * mine
+    buckets = 2 * chans * 3
+
+    def inside(x, count):
+        return (x >= 0) & (x < count)
+
+    def keys(code, index, q_b):
+        def field(at, bits=2):
+            return lax.shift_right_logical(code, at) & ((1 << bits) - 1)
+
+        out_b, out_a, in_b, in_a = (field(2 * j) - 1 for j in range(4))
+        s, sp, w_in, w_out = field(8), field(10), field(12, 5), field(17, 5)
+        up_a, up_b = s & 1, lax.shift_right_logical(s, 1)
+        i = w_out - row * chans
+        to_b = up_b + out_b + q_b
+        live = (inside(i, chans) & inside(up_b + q_b, sec_b) & inside(up_a + a, sec_a)
+                & inside(in_b + q_b, sec_b) & inside(in_a + a, sec_a)
+                & inside(up_a + out_a + a, sec_a) & inside(to_b, sec_b))
+        key = jnp.where(live, (up_a * chans + i) * 3 + jnp.where(up_b == 0, q_b, 2), buckets)
+        pack = (w_in * 2 + q_b) * 32 + (up_a + out_a + 1) * 8 + sp * 2 + to_b
+        return key, key * (2 * wide) + q_b * wide + index, pack
+
+    total = jnp.sum(held[:, 0:8, :], axis=0).astype(jnp.int32)
+    lane = lax.broadcasted_iota(jnp.int32, (1, 128), 1)
+    along = [keys(total[c:c + 1], lane + 128 * c, q)[1] for c in range(wide // 128) for q in (0, 1)]
+    code = held[:, 8:8 + mine, :].reshape(wide, 128).astype(jnp.int32)
+    value = held[:, 8 + mine:8 + 2 * mine, :].reshape(wide, 128)
+    index = lax.broadcasted_iota(jnp.int32, (wide, 128), 0)
+    lanes = lax.broadcasted_iota(jnp.int32, (wide, 128), 1)
+    starts = jnp.zeros((1, 128), jnp.int32)
+    packs = [jnp.zeros((1, 128), jnp.float32) for _ in range(2 * wide // 128)]
+    values = [jnp.zeros((1, 128), jnp.float32) for _ in range(2 * wide // 128)]
+    for q in (0, 1):
+        key, order, pack = keys(code, index, q)
+        starts += jnp.sum(jnp.where(key < lanes, 1.0, 0.0), axis=0, keepdims=True).astype(jnp.int32)
+        before = jnp.zeros((wide, 128), jnp.float32)
+        for other in along:
+            before += jnp.where(other < order, 1.0, 0.0)
+        rank = jnp.sum(before, axis=1, keepdims=True).astype(jnp.int32)
+        pack = pack.astype(jnp.float32)
+        for c in range(len(packs)):
+            hit = rank == lanes + 128 * c
+            packs[c] += jnp.sum(jnp.where(hit, pack, 0.0), axis=0, keepdims=True)
+            values[c] += jnp.sum(jnp.where(hit, value, 0.0), axis=0, keepdims=True)
+    for c in range(len(packs)):
+        ints[c:c + 1, :] = packs[c].astype(jnp.int32)
+        floats[c:c + 1, :] = values[c]
+    ints[4:5, :] = starts
+
+
+def gather_kernel(n, chans, sec_a, sec_b, sizes, env, bra_hbm, info, env_all, bra_all, info_all, ints, floats,
+                  info_own, env_own, bra_raw, bra, send, recv, isend, irecv, bsend, brecv, local):
     a = lax.axis_index("sec")
     row = lax.axis_index("row")
     pos = ring_pos(row, n)
@@ -139,8 +206,9 @@
 
     for way in (0, 1):
         info_copy(1, way, row).start()
-    for b in range(blocks):
+    for at in range(blocks):
         for way in (0, 1):
+            b = blocks - 1 - at if way else at
             if used(1, way, b):
                 @pl.when(carried(1, way, b, row))
                 def _(b=b, way=way):
@@ -151,8 +219,6 @@
     )
     for copy in loads:
         copy.start()
-    info_own = pltpu.make_async_copy(info, info_all.at[row], local.at[2])
-    info_own.start()
 
     def size_at(x, y):
         inner = jnp.where((x >= 0) & (y >= 0), sizes[jnp.maximum(x, 0) * sec_b + max(y, 0)], 0)
@@ -174,9 +240,8 @@
     own = (
         pltpu.make_async_copy(env_own, env_all.at[pl.ds(row * blocks, blocks)], local.at[1]),
         pltpu.make_async_copy(bra, bra_all.at[1], local.at[0]),
-        info_own,
     )
-    for copy in own[:2]:
+    for copy in own:
         copy.start()
 
     for k in range(1, hops + 1):
@@ -186,8 +251,11 @@
                 info_copy(k, way, sources[way]).wait_recv()
                 if k < half and info_used(k + 1, way):
                     info_copy(k + 1, way, sources[way]).start()
-        for b in range(blocks):
+        if k == half:
+            fill_lists(n, chans, sec_a, sec_b, a, row, info, info_all, info_own, ints, floats, local.at[2])
+        for at in range(blocks):
             for way in (0, 1):
+                b = blocks - 1 - at if way else at
                 if used(k, way, b):
                     @pl.when(carried(k, way, b, sources[way]))
                     def _(k=k, way=way, b=b):
@@ -230,11 +298,13 @@
             jax.ShapeDtypeStruct((n * blocks,) + env.shape[1:], env.dtype),
             jax.ShapeDtypeStruct((4,) + bra.shape, bra.dtype),
             jax.ShapeDtypeStruct((n,) + info.shape, info.dtype),
+            jax.ShapeDtypeStruct((8, 128), jnp.int32),
+            jax.ShapeDtypeStruct((8, 128), jnp.float32),
         ),
         in_specs=[pl.BlockSpec(memory_space=pltpu.SMEM)] + [anywhere] * 3,
-        out_specs=(anywhere,) * 3,
+        out_specs=(anywhere,) * 3 + (pl.BlockSpec(memory_space=pltpu.VMEM),) * 2,
         scratch_shapes=[
-            pltpu.VMEM(env.shape, env.dtype), pltpu.VMEM(bra.shape, bra.dtype), pltpu.VMEM(bra.shape, bra.dtype),
+            pltpu.VMEM((n,) + info.shape, info.dtype), pltpu.VMEM(env.shape, env.dtype), pltpu.VMEM(bra.shape, bra.dtype), pltpu.VMEM(bra.shape, bra.dtype),
             dma((hops, 2, blocks)), dma((hops, 2, blocks)), dma((half, 2)), dma((half, 2)),
             dma((3,)), dma((3,)), dma((3,)),
         ],
@@ -244,38 +314,35 @@
     )(sizes, env, bra, info)
 
 
-def terms_kernel(up_a, base, count, starts, packed, values, ksz, env, bra_hbm, ket_hbm, out,
-                 buf, bra, ket, t_acc, acc, sems, load):
-    first = starts[base * 3]
-    last = starts[(base + count) * 3]
-    loads = [pltpu.make_async_copy(bra_hbm.at[pl.ds(8 * up_a, 24)], bra, load.at[0])]
-    loads += [
-        pltpu.make_async_copy(ket_hbm.at[(up_a + 2 * (j // 2)) * 2 + j % 2], ket.at[j], load.at[1 + j])
-        for j in range(3)
-    ]
-    loads[0].start()
+def terms_kernel(up_a, base, count, sec_a, ints, floats, ksz, env, bra, ket, out,
+                 buf, t_acc, acc, sems):
+    a = lax.axis_index("sec")
+    to_a = jnp.minimum(a + up_a, sec_a - 1)
+
+    def at(j):
+        return ints[lax.div(j, 128), lax.rem(j, 128)]
+
+    def start(bucket):
+        return ints[4, bucket]
+
+    first, last = start(base * 3), start((base + count) * 3)
 
     def fetch(j):
         slot = lax.rem(j, DEPTH)
-        return pltpu.make_async_copy(env.at[lax.div(packed[j], 32)], buf.at[slot], sems.at[slot])
+        return pltpu.make_async_copy(env.at[lax.div(at(j), 32)], buf.at[slot], sems.at[slot])
 
     for d in range(DEPTH):
         @pl.when(first + d < last)
         def _(d=d):
             fetch(first + d).start()
 
-    for copy in loads[1:]:
-        copy.start()
     acc[...] = jnp.zeros_like(acc)
     cols = lax.broadcasted_iota(jnp.int32, t_acc.shape, 1)
-
-    for copy in loads:
-        copy.wait()
 
     def channel(i, carry):
         for kind, (up_b, q_b) in enumerate(((0, 0), (0, 1), (1, 0))):
             bucket = (base + i) * 3 + kind
-            begin, end = starts[bucket], starts[bucket + 1]
+            begin, end = start(bucket), start(bucket + 1)
 
             @pl.when(end > begin)
             def _():
@@ -283,9 +350,9 @@
 
                 def item(j, c):
                     fetch(j).wait()
-                    b = bra[lax.rem(packed[j], 32) - 8 * up_a]
+                    b = bra[lax.rem(at(j), 32)]
                     e = buf[lax.rem(j, DEPTH)]
-                    t_acc[...] += values[j] * jnp.dot(b, e, preferred_element_type=jnp.float32)
+                    t_acc[...] += floats[lax.div(j, 128), lax.rem(j, 128)] * jnp.dot(b, e, preferred_element_type=jnp.float32)
 
                     @pl.when(j + DEPTH < last)
                     def _():
@@ -293,39 +360,37 @@
                     return c
 
                 lax.fori_loop(begin, end, item, 0)
-                t = jnp.where(cols < ksz[q_b], t_acc[...], 0.0).astype(jnp.bfloat16)
-                k = ket[2 * up_b + q_b]
+                t = jnp.where(cols < ksz[a * 2 + q_b], t_acc[...], 0.0).astype(jnp.bfloat16)
+                k = ket[(up_a + 2 * up_b) * 2 + q_b]
                 acc[i * 2 + up_b + q_b] += jnp.dot(t, k, preferred_element_type=jnp.float32)
         for p_b in (0, 1):
             block = acc[i * 2 + p_b]
-            out[i * 2 + p_b] = jnp.where(cols < ksz[2 + p_b], block, 0.0).astype(out.dtype)
+            out[i * 2 + p_b] = jnp.where(cols < ksz[to_a * 2 + p_b], block, 0.0).astype(out.dtype)
         return carry
 
     lax.fori_loop(0, count, channel, 0)
 
 
-def terms(up_a, chans, at, count, starts, packed, values, ksz, env, bra, ket, dtype):
+def terms(up_a, chans, at, count, sec_a, ints, floats, ksz, env, bra, ket, dtype):
     rows, cols = env.shape[1:]
     blocks = count * 2
     smem = pl.BlockSpec(memory_space=pltpu.SMEM)
+    vmem = pl.BlockSpec(memory_space=pltpu.VMEM)
     return pl.pallas_call(
-        functools.partial(terms_kernel, up_a, up_a * chans + at, count),
+        functools.partial(terms_kernel, up_a, up_a * chans + at, count, sec_a),
         out_shape=jax.ShapeDtypeStruct((blocks, rows, cols), dtype),
-        in_specs=[smem] * 4 + [pl.BlockSpec(memory_space=pl.ANY)] * 3,
+        in_specs=[smem] * 3 + [pl.BlockSpec(memory_space=pl.ANY), vmem, vmem],
         out_specs=pl.BlockSpec(memory_space=pltpu.VMEM),
         scratch_shapes=[
             pltpu.VMEM((DEPTH, rows, cols), env.dtype),
-            pltpu.VMEM((24,) + bra.shape[1:], bra.dtype),
-            pltpu.VMEM((3,) + ket.shape[1:], ket.dtype),
             pltpu.VMEM((rows, cols), jnp.float32),
             pltpu.VMEM((blocks, rows, cols), jnp.float32),
             pltpu.SemaphoreType.DMA((DEPTH,)),
-            pltpu.SemaphoreType.DMA((4,)),
         ],
-        compiler_params=pltpu.CompilerParams(vmem_limit_bytes=60 * 1024 * 1024),
+        compiler_params=pltpu.CompilerParams(vmem_limit_bytes=40 * 1024 * 1024),
         cost_estimate=pl.CostEstimate(flops=5 * 10**9, bytes_accessed=16 * 2**20, transcendentals=0),
         name="terms_up" if up_a else "terms_same",
-    )(starts, packed, values, ksz, env, bra, ket)
+    )(ints, floats, ksz, env, bra, ket)
 
 
 def body(env_in, ket_mps, bra_mps, ket_sizes, bra_sizes, entries, coeffs):
@@ -333,61 +398,34 @@
     a = lax.axis_index("sec")
     row = lax.axis_index("row")
     sec_a, n = lax.axis_size("sec"), lax.axis_size("row")
-    ket_ext = jnp.pad(ket_sizes, 1)
-
-    def sizes_at(ext, pad, shift_a, shift_b):
-        return lax.dynamic_slice(ext, (a + shift_a + pad, jnp.int32(shift_b + pad)), (1, sec_b))[0]
-
     bra = bra_mps.reshape(4 * sec_b, bra_w, bra_w)
-    code = (entries[..., 0] * 16 + entries[..., 1] * 4 + entries[..., 2]).astype(jnp.float32)
-    mine = chans * EPW
-    info = jnp.pad(jnp.stack([code.reshape(-1), coeffs.reshape(-1)]), ((0, 6), (0, 128 - mine)))
-
-    env_all, bra_all, info_all = gather(
+    mine, wide = chans * EPW, n * chans * EPW
+    w_in = (row * chans + jnp.arange(chans, dtype=jnp.int32))[:, None]
+    in_a, in_b = channel_charge(w_in)
+    out_a, out_b = channel_charge(entries[..., 0])
+    code = entries[..., 0] * 32 + w_in
+    for field in (entries[..., 1], entries[..., 2], in_a + 1, in_b + 1, out_a + 1, out_b + 1):
+        code = code * 4 + field
+    code = code.reshape(-1).astype(jnp.float32)
+    lanes = lax.dynamic_update_slice(jnp.zeros((wide,), jnp.float32), code, (row * mine,)).reshape(-1, 128)
+    info = jnp.concatenate([
+        jnp.pad(lanes, ((0, 8 - lanes.shape[0]), (0, 0))),
+        jnp.broadcast_to(code[:, None], (mine, 128)),
+        jnp.broadcast_to(coeffs.reshape(-1)[:, None], (mine, 128)),
+    ])
+
+    env_all, bra_all, _, ints, floats = gather(
         bra_sizes.reshape(-1), env_in.reshape(chans * sec_b, bra_w, ket_w), bra, info, n, chans, sec_a, sec_b)
     bra_all = bra_all.reshape(4 * 4 * sec_b, bra_w, bra_w)
 
-    code = info_all[:, 0, :mine].reshape(-1).astype(jnp.int32)
-    value = info_all[:, 1, :mine].reshape(-1)
-    wide = code.shape[0]
-    code, value = jnp.tile(code, 2), jnp.tile(value, 2)
-    index = jnp.arange(2 * wide, dtype=jnp.int32)
-    q_b = index // wide
-    w_in = (index % wide) // EPW
-    w_out, sp, s = code // 16, (code // 4) % 4, code % 4
-    up_a, up_b = s % 2, s // 2
-    in_a, in_b = channel_charge(w_in)
-    out_a, out_b = channel_charge(w_out)
-    i = w_out - row * chans
-    to_a, to_b = a + up_a + out_a, q_b + up_b + out_b
-
-    def inside(x, count):
-        return (x >= 0) & (x < count)
-
-    live = (inside(i, chans) & inside(q_b + up_b, sec_b) & inside(a + up_a, sec_a)
-            & inside(q_b + in_b, sec_b) & inside(a + in_a, sec_a)
-            & inside(to_a, sec_a) & inside(to_b, sec_b))
-    buckets = 2 * chans * 3
-    key = jnp.where(live, (up_a * chans + i) * 3 + jnp.where(up_b == 0, q_b, 2), buckets)
-    pack = (w_in * 2 + q_b) * 32 + (up_a + out_a + 1) * 8 + sp * 2 + to_b
-    starts = jnp.sum(key[None, :] < jnp.arange(buckets + 1, dtype=jnp.int32)[:, None], axis=1, dtype=jnp.int32)
-    order = key * (2 * wide) + index
-    rank = jnp.sum(order[None, :] < order[:, None], axis=1, dtype=jnp.int32)
-    hit = rank[None, :] == index[:, None]
-    packed = jnp.sum(jnp.where(hit, pack[None, :], 0), axis=1, dtype=jnp.int32)
-    values = jnp.sum(jnp.where(hit, value[None, :], 0.0), axis=1)
-
     ket = ket_mps.reshape(4 * sec_b, ket_w, ket_w)
-    here = sizes_at(ket_ext, 1, 0, 0)
-    above = sizes_at(ket_ext, 1, 1, 0)
+    ksz = ket_sizes.reshape(-1)
     sent = []
     part = chans // 2
     for at in (0, part):
-        up = terms(1, chans, at, part, starts, packed, values, jnp.concatenate([here, above]),
-                   env_all, bra_all, ket, jnp.bfloat16)
+        up = terms(1, chans, at, part, sec_a, ints, floats, ksz, env_all, bra_all, ket, jnp.bfloat16)
         sent.append(lax.ppermute(up, "sec", [(k, k + 1) for k in range(sec_a - 1)]))
-    same = terms(0, chans, 0, chans, starts, packed, values, jnp.concatenate([here, here]),
-                 env_all, bra_all, ket, jnp.float32)
+    same = terms(0, chans, 0, chans, sec_a, ints, floats, ksz, env_all, bra_all, ket, jnp.float32)
     out = (same + jnp.concatenate(sent).astype(jnp.float32)).astype(env_in.dtype)
     return out.reshape(env_in.shape)
 

time: 171 us -> 162 us (0.947)
  the two profiles are of different devices: /device:TPU:22 before, /device:TPU:1 now
where the time goes in v4:
time: 162 us
  Pallas kernels  130 us (80%)
  starting transfers between devices  11.3 us (7%)
  local copies, waits for them, and re-layouts  9.71 us (6%)
  waiting for transfers between devices  8.01 us (5%)
  other arithmetic  3.69 us (2%)
    pallas_call x1, Pallas kernels, gather(): pl.pallas_call(functools.partial(gather_kernel, n, chans, sec_a, sec_b),...  112 us
    pallas_call x3, Pallas kernels, terms(): pl.pallas_call(functools.partial(terms_kernel, up_a, up_a * chans + at, c...  17.5 us
    ppermute x2, starting transfers between devices, body(): sent.append(lax.ppermute(up, 'sec', [(k, k + 1) for k in range(sec_a - 1)]))  11.3 us
    ppermute x2, waiting for transfers between devices, body(): sent.append(lax.ppermute(up, 'sec', [(k, k + 1) for k in range(sec_a - 1)]))  8.01 us
    unnamed x10, local copies, waits for them, and re-layouts  7.25 us
  transfers between devices with their start and end apart: 2, of which 1 were waited for; matrix products, arithmetic and copies ran while one was open for 0% of the time, Pallas kernels for 8%

profile of v4, /device:TPU:1, one launch (start us, length us, event | category | flops | bytes accessed | tf_op | source)
XLA Modules:
  0.0 162.5 jit_solution(3818777493929783361)
XLA Ops:
  0.0 0.8 reshape.116
  0.9 0.1 add.152
  1.0 0.1 add.157
  1.2 0.1 add.160
  1.3 0.8 copy.12
  2.0 0.1 reshape.111.ksz
  2.1 0.8 copy.11
  2.9 0.6 reshape.107.sizes
  3.5 0.7 slice_multiply_fusion
  4.2 0.1 mul.70
  4.7 0.1 fusion.1
  4.9 0.7 fusion.info
  5.6 112.2 %gather_row.1 = (bf16[64,256,512]{2,1,0:T(8,128)(2,1)}, bf16[4,8,256,256]{3,2,1,0:T(8,128)(2,1)}, f32[8,72,128]{2,1,0:T(8,128)}, s32[8,128]{1,0:T(8,128)}, f32[8,128]{1,0:T(8,128)}) custom-call(s32[8]{0:T(128)} %reshape.107.sizes, bf16[8,256,512]{2,1,0:T(8,128)(2,1)} %bitcast.24, bf16[8,256,256]{2,1,0:T(8,128)(2,1)} %bitcast.25, f32[72,128]{1,0:T(8,128)} %fusion.info), custom_call_target="tpu_custom_call" | custom-call | tf_op jit(solution)/shard_map/gather_row/pallas_call | solution.py:295
  117.8 2.2 %copy-done = bf16[4,1,2,512,512]{4,3,2,1,0:T(8,128)(2,1)S(1)} copy-done((bf16[4,1,2,512,512]{4,3,2,1,0:T(8,128)(2,1)S(1)}, bf16[4,1,2,512,512]{4,3,2,1,0:T(8,128)(2,1)}, u32[]{:S(2)}) %copy-start) | copy-done | bytes 4194328
  120.0 2.2 %copy-done.1 = bf16[4,8,256,256]{3,2,1,0:T(8,128)(2,1)S(1)} copy-done((bf16[4,8,256,256]{3,2,1,0:T(8,128)(2,1)S(1)}, bf16[4,8,256,256]{3,2,1,0:T(8,128)(2,1)}, u32[]{:S(2)}) %copy-start.1) | copy-done | bytes 4194328
  122.2 0.7 copy-done.2
  122.9 0.7 copy-done.3
  123.5 4.5 %terms_up.2 = bf16[4,256,512]{2,1,0:T(8,128)(2,1)S(1)} custom-call(s32[8,128]{1,0:T(8,128)S(1)} %copy-done.2, f32[8,128]{1,0:T(8,128)S(1)} %copy-done.3, s32[8]{0:T(128)S(1)} %reshape.111.ksz, bf16[64,256,512]{2,1,0:T(8,128)(2,1)} %get-tuple-element.11.env, bf16[32,256,256]{2,1,0:T(8,128)(2,1)S(1)} %bitcast.21, bf16[8,512,512]{2,1,0:T(8,128)(2,1)S(1)} %bitcast.18), custom_call_target="tpu_custom_call" | custom-call | flops 5000000000 | bytes 16777216 | tf_op jit(solution)/shard_map/terms_up/pallas_call | solution.py:379
  128.0 9.4 %collective-permute-start = (bf16[4,256,512]{2,1,0:T(8,128)(2,1)S(1)}, bf16[4,256,512]{2,1,0:T(8,128)(2,1)S(1)}, u32[]{:S(2)}, u32[]{:S(2)}) collective-permute-start(bf16[4,256,512]{2,1,0:T(8,128)(2,1)S(1)} %terms_up.2), channel_id=1, source_target_pairs={{0,8},{8,16},{16,24},{1,9},{9,17},{17,25},{2,10},{10,18},{18,26},{... | collective-permute-start | bytes 3145736 | tf_op jit(solution)/shard_map/ppermute | solution.py:427
  137.4 5.3 %terms_up.3 = bf16[4,256,512]{2,1,0:T(8,128)(2,1)S(1)} custom-call(s32[8,128]{1,0:T(8,128)S(1)} %copy-done.2, f32[8,128]{1,0:T(8,128)S(1)} %copy-done.3, s32[8]{0:T(128)S(1)} %reshape.111.ksz, bf16[64,256,512]{2,1,0:T(8,128)(2,1)} %get-tuple-element.11.env, bf16[32,256,256]{2,1,0:T(8,128)(2,1)S(1)} %bitcast.22, bf16[8,512,512]{2,1,0:T(8,128)(2,1)S(1)} %bitcast.19), custom_call_target="tpu_custom_call" | custom-call | flops 5000000000 | bytes 16777216 | tf_op jit(solution)/shard_map/terms_up/pallas_call | solution.py:379
  142.7 1.9 %collective-permute-start.1 = (bf16[4,256,512]{2,1,0:T(8,128)(2,1)S(1)}, bf16[4,256,512]{2,1,0:T(8,128)(2,1)S(1)}, u32[]{:S(2)}, u32[]{:S(2)}) collective-permute-start(bf16[4,256,512]{2,1,0:T(8,128)(2,1)S(1)} %terms_up.3), channel_id=1, source_target_pairs={{0,8},{8,16},{16,24},{1,9},{9,17},{17,25},{2,10},{10,18},{18,26},{... | collective-permute-start | bytes 3145736 | tf_op jit(solution)/shard_map/ppermute | solution.py:427
  144.6 7.7 %terms_same.1 = f32[8,256,512]{2,1,0:T(8,128)S(1)} custom-call(s32[8,128]{1,0:T(8,128)S(1)} %copy-done.2, f32[8,128]{1,0:T(8,128)S(1)} %copy-done.3, s32[8]{0:T(128)S(1)} %reshape.111.ksz, bf16[64,256,512]{2,1,0:T(8,128)(2,1)} %get-tuple-element.11.env, bf16[32,256,256]{2,1,0:T(8,128)(2,1)S(1)} %bitcast.23, bf16[8,512,512]{2,1,0:T(8,128)(2,1)S(1)} %bitcast.20), custom_call_target="tpu_custom_call" | custom-call | flops 5000000000 | bytes 16777216 | tf_op jit(solution)/shard_map/terms_same/pallas_call | solution.py:379
  152.4 8.0 %collective-permute-done.1 = bf16[4,256,512]{2,1,0:T(8,128)(2,1)S(1)} collective-permute-done((bf16[4,256,512]{2,1,0:T(8,128)(2,1)S(1)}, bf16[4,256,512]{2,1,0:T(8,128)(2,1)S(1)}, u32[]{:S(2)}, u32[]{:S(2)}) %collective-permute-start.1) | collective-permute-done | bytes 1048608 | tf_op jit(solution)/shard_map/ppermute | solution.py:427
  160.4 2.1 %add_convert_fusion = bf16[8,256,512]{2,1,0:T(8,128)(2,1)} fusion(f32[8,256,512]{2,1,0:T(8,128)S(1)} %terms_same.1, bf16[4,256,512]{2,1,0:T(8,128)(2,1)S(1)} %collective-permute-done.1, bf16[4,256,512]{2,1,0:T(8,128)(2,1)S(1)} %collective-permute-done), kind=kLoop, calls=%fused_computation | loop fusion | flops 4194304 | bytes 8388608 | tf_op jit(solution)/shard_map/convert_element_type | solution.py:429
  (17 shorter events, 0.7 us)
Async XLA Ops:
  117.8 2.2 %copy-start = (bf16[4,1,2,512,512]{4,3,2,1,0:T(8,128)(2,1)S(1)}, bf16[4,1,2,512,512]{4,3,2,1,0:T(8,128)(2,1)}, u32[]{:S(2)}) copy-start(bf16[4,1,2,512,512]{4,3,2,1,0:T(8,128)(2,1)} %param.8) | copy-start | bytes 12582916
  120.0 2.2 %copy-start.1 = (bf16[4,8,256,256]{3,2,1,0:T(8,128)(2,1)S(1)}, bf16[4,8,256,256]{3,2,1,0:T(8,128)(2,1)}, u32[]{:S(2)}) copy-start(bf16[4,8,256,256]{3,2,1,0:T(8,128)(2,1)} %get-tuple-element.12) | copy-start | bytes 12582916
  122.2 0.7 copy-start.2
  122.9 0.7 copy-start.3
  128.0 24.3 %collective-permute-start = (bf16[4,256,512]{2,1,0:T(8,128)(2,1)S(1)}, bf16[4,256,512]{2,1,0:T(8,128)(2,1)S(1)}, u32[]{:S(2)}, u32[]{:S(2)}) collective-permute-start(bf16[4,256,512]{2,1,0:T(8,128)(2,1)S(1)} %terms_up.2), channel_id=1, source_target_pairs={{0,8},{8,16},{16,24},{1,9},{9,17},{17,25},{2,10},{10,18},{18,26},{... | collective-permute-start | bytes 3145736 | tf_op jit(solution)/shard_map/ppermute | solution.py:427
  142.7 17.7 %collective-permute-start.1 = (bf16[4,256,512]{2,1,0:T(8,128)(2,1)S(1)}, bf16[4,256,512]{2,1,0:T(8,128)(2,1)S(1)}, u32[]{:S(2)}, u32[]{:S(2)}) collective-permute-start(bf16[4,256,512]{2,1,0:T(8,128)(2,1)S(1)} %terms_up.3), channel_id=1, source_target_pairs={{0,8},{8,16},{16,24},{1,9},{9,17},{17,25},{2,10},{10,18},{18,26},{... | collective-permute-start | bytes 3145736 | tf_op jit(solution)/shard_map/ppermute | solution.py:427

commit v5 on v4

--- a/solution.py
+++ b/solution.py
@@ -147,7 +147,7 @@
 
 
 def gather_kernel(n, chans, sec_a, sec_b, sizes, env, bra_hbm, info, env_all, bra_all, info_all, ints, floats,
-                  info_own, env_own, bra_raw, bra, send, recv, isend, irecv, bsend, brecv, local):
+                  info_own, env_own, bra_raw, bra, send, recv, isend, irecv, bsend, brecv, local, go):
     a = lax.axis_index("sec")
     row = lax.axis_index("row")
     pos = ring_pos(row, n)
@@ -206,13 +206,21 @@
 
     for way in (0, 1):
         info_copy(1, way, row).start()
-    for at in range(blocks):
-        for way in (0, 1):
-            b = blocks - 1 - at if way else at
-            if used(1, way, b):
-                @pl.when(carried(1, way, b, row))
-                def _(b=b, way=way):
-                    block_copy(1, way, b, row).start()
+    staged = sec_a >= 4
+
+    def first_hop():
+        for at in range(blocks):
+            for way in (0, 1):
+                b = blocks - 1 - at if way else at
+                if used(1, way, b):
+                    @pl.when(carried(1, way, b, row))
+                    def _(b=b, way=way):
+                        block_copy(1, way, b, row).start()
+
+    if staged:
+        pl.when((a > 0) & (a < sec_a - 1))(first_hop)
+    else:
+        first_hop()
     loads = (
         pltpu.make_async_copy(bra_hbm, bra_raw, local.at[0]),
         pltpu.make_async_copy(env, env_own, local.at[1]),
@@ -243,6 +251,11 @@
     )
     for copy in own:
         copy.start()
+    if staged:
+        @pl.when((a == 0) | (a == sec_a - 1))
+        def _():
+            pl.semaphore_wait(go, 1)
+            first_hop()
 
     for k in range(1, hops + 1):
         sources = [source_at(k, way) for way in (0, 1)]
@@ -264,6 +277,11 @@
                             @pl.when(carried(k + 1, way, b, sources[way]))
                             def _():
                                 block_copy(k + 1, way, b, sources[way]).start()
+        if staged and k == half // 2:
+            for inner, edge in ((1, 0), (sec_a - 2, sec_a - 1)):
+                @pl.when(a == inner)
+                def _(edge=edge):
+                    pl.semaphore_signal(go, inc=1, device_id={"sec": edge}, device_id_type=MESH)
 
     for k in range(1, hops + 1):
         for way in (0, 1):
@@ -306,10 +324,10 @@
         scratch_shapes=[
             pltpu.VMEM((n,) + info.shape, info.dtype), pltpu.VMEM(env.shape, env.dtype), pltpu.VMEM(bra.shape, bra.dtype), pltpu.VMEM(bra.shape, bra.dtype),
             dma((hops, 2, blocks)), dma((hops, 2, blocks)), dma((half, 2)), dma((half, 2)),
-            dma((3,)), dma((3,)), dma((3,)),
+            dma((3,)), dma((3,)), dma((3,)), pltpu.SemaphoreType.REGULAR,
         ],
         compiler_params=pltpu.CompilerParams(
-            collective_id=0, has_side_effects=True, vmem_limit_bytes=60 * 1024 * 1024),
+            collective_id=0, has_side_effects=True, vmem_limit_bytes=54 * 1024 * 1024),
         name="gather_row",
     )(sizes, env, bra, info)
 
@@ -387,7 +405,7 @@
             pltpu.VMEM((blocks, rows, cols), jnp.float32),
             pltpu.SemaphoreType.DMA((DEPTH,)),
         ],
-        compiler_params=pltpu.CompilerParams(vmem_limit_bytes=40 * 1024 * 1024),
+        compiler_params=pltpu.CompilerParams(vmem_limit_bytes=28 * 1024 * 1024),
         cost_estimate=pl.CostEstimate(flops=5 * 10**9, bytes_accessed=16 * 2**20, transcendentals=0),
         name="terms_up" if up_a else "terms_same",
     )(ints, floats, ksz, env, bra, ket)
@@ -420,13 +438,10 @@
 
     ket = ket_mps.reshape(4 * sec_b, ket_w, ket_w)
     ksz = ket_sizes.reshape(-1)
-    sent = []
-    part = chans // 2
-    for at in (0, part):
-        up = terms(1, chans, at, part, sec_a, ints, floats, ksz, env_all, bra_all, ket, jnp.bfloat16)
-        sent.append(lax.ppermute(up, "sec", [(k, k + 1) for k in range(sec_a - 1)]))
+    up = terms(1, chans, 0, chans, sec_a, ints, floats, ksz, env_all, bra_all, ket, jnp.bfloat16)
+    up = lax.ppermute(up, "sec", [(k, k + 1) for k in range(sec_a - 1)])
     same = terms(0, chans, 0, chans, sec_a, ints, floats, ksz, env_all, bra_all, ket, jnp.float32)
-    out = (same + jnp.concatenate(sent).astype(jnp.float32)).astype(env_in.dtype)
+    out = (same + up.astype(jnp.float32)).astype(env_in.dtype)
     return out.reshape(env_in.shape)
 
 

time: 162 us -> 147 us (0.907)
  the two profiles are of different devices: /device:TPU:1 before, /device:TPU:30 now
where the time goes in v5:
time: 147 us; the launch traced here: 144 us
  Pallas kernels  108 us (73%)
  starting transfers between devices  22.4 us (15%)
  local copies, waits for them, and re-layouts  9.79 us (7%)
  other arithmetic  3.7 us (3%)
    pallas_call x1, Pallas kernels, gather(): pl.pallas_call(functools.partial(gather_kernel, n, chans, sec_a, sec_b),...  93.8 us
    ppermute x1, starting transfers between devices, body(): up = lax.ppermute(up, 'sec', [(k, k + 1) for k in range(sec_a - 1)])  22.4 us
    pallas_call x2, Pallas kernels, terms(): pl.pallas_call(functools.partial(terms_kernel, up_a, up_a * chans + at, c...  14.1 us
    unnamed x10, local copies, waits for them, and re-layouts  7.26 us
  transfers between devices with their start and end apart: 1, of which 0 were waited for; matrix products, arithmetic and copies ran while one was open for 0% of the time, Pallas kernels for 5%

profile of v5, /device:TPU:30, one launch (start us, length us, event | category | flops | bytes accessed | tf_op | source)
XLA Modules:
  0.0 143.8 jit_solution(15777909123059886906)
XLA Ops:
  0.0 0.8 reshape.116
  0.9 0.1 add.152
  1.0 0.1 add.157
  1.2 0.1 add.160
  1.3 0.8 copy.12
  2.0 0.1 reshape.111.ksz
  2.1 0.8 copy.11
  2.9 0.7 reshape.107.sizes
  3.5 0.7 slice_multiply_fusion
  4.3 0.1 mul.70
  4.4 0.1 rem.47
  4.4 0.1 div.21
  4.5 0.1 squeeze.9
  4.8 0.1 fusion.1
  4.9 0.7 fusion.info
  5.7 93.8 %gather_row.1 = (bf16[64,256,512]{2,1,0:T(8,128)(2,1)}, bf16[4,8,256,256]{3,2,1,0:T(8,128)(2,1)}, f32[8,72,128]{2,1,0:T(8,128)}, s32[8,128]{1,0:T(8,128)}, f32[8,128]{1,0:T(8,128)}) custom-call(s32[8]{0:T(128)} %reshape.107.sizes, bf16[8,256,512]{2,1,0:T(8,128)(2,1)} %bitcast.22, bf16[8,256,256]{2,1,0:T(8,128)(2,1)} %bitcast.23, f32[72,128]{1,0:T(8,128)} %fusion.info), custom_call_target="tpu_custom_call" | custom-call | tf_op jit(solution)/shard_map/gather_row/pallas_call | solution.py:313
  99.4 2.2 %copy-done = bf16[4,1,2,512,512]{4,3,2,1,0:T(8,128)(2,1)S(1)} copy-done((bf16[4,1,2,512,512]{4,3,2,1,0:T(8,128)(2,1)S(1)}, bf16[4,1,2,512,512]{4,3,2,1,0:T(8,128)(2,1)}, u32[]{:S(2)}) %copy-start) | copy-done | bytes 4194328
  101.6 2.2 %copy-done.1 = bf16[4,8,256,256]{3,2,1,0:T(8,128)(2,1)S(1)} copy-done((bf16[4,8,256,256]{3,2,1,0:T(8,128)(2,1)S(1)}, bf16[4,8,256,256]{3,2,1,0:T(8,128)(2,1)}, u32[]{:S(2)}) %copy-start.1) | copy-done | bytes 4194328
  103.8 0.7 copy-done.2
  104.5 0.7 copy-done.3
  105.2 6.6 %terms_up.1 = bf16[8,256,512]{2,1,0:T(8,128)(2,1)S(1)} custom-call(s32[8,128]{1,0:T(8,128)S(1)} %copy-done.2, f32[8,128]{1,0:T(8,128)S(1)} %copy-done.3, s32[8]{0:T(128)S(1)} %reshape.111.ksz, bf16[64,256,512]{2,1,0:T(8,128)(2,1)} %get-tuple-element.11.env, bf16[32,256,256]{2,1,0:T(8,128)(2,1)S(1)} %bitcast.20, bf16[8,512,512]{2,1,0:T(8,128)(2,1)S(1)} %bitcast.18), custom_call_target="tpu_custom_call" | custom-call | flops 5000000000 | bytes 16777216 | tf_op jit(solution)/shard_map/terms_up/pallas_call | solution.py:397
  111.8 22.4 %collective-permute-start = (bf16[8,256,512]{2,1,0:T(8,128)(2,1)S(1)}, bf16[8,256,512]{2,1,0:T(8,128)(2,1)S(1)}, u32[]{:S(2)}, u32[]{:S(2)}) collective-permute-start(bf16[8,256,512]{2,1,0:T(8,128)(2,1)S(1)} %terms_up.1), channel_id=1, source_target_pairs={{0,8},{8,16},{16,24},{1,9},{9,17},{17,25},{2,10},{10,18},{18,26},{... | collective-permute-start | bytes 6291464 | tf_op jit(solution)/shard_map/ppermute | solution.py:442
  134.2 7.5 %terms_same.1 = f32[8,256,512]{2,1,0:T(8,128)S(1)} custom-call(s32[8,128]{1,0:T(8,128)S(1)} %copy-done.2, f32[8,128]{1,0:T(8,128)S(1)} %copy-done.3, s32[8]{0:T(128)S(1)} %reshape.111.ksz, bf16[64,256,512]{2,1,0:T(8,128)(2,1)} %get-tuple-element.11.env, bf16[32,256,256]{2,1,0:T(8,128)(2,1)S(1)} %bitcast.21, bf16[8,512,512]{2,1,0:T(8,128)(2,1)S(1)} %bitcast.19), custom_call_target="tpu_custom_call" | custom-call | flops 5000000000 | bytes 16777216 | tf_op jit(solution)/shard_map/terms_same/pallas_call | solution.py:397
  141.7 2.1 %add_convert_fusion = bf16[8,256,512]{2,1,0:T(8,128)(2,1)} fusion(f32[8,256,512]{2,1,0:T(8,128)S(1)} %terms_same.1, bf16[8,256,512]{2,1,0:T(8,128)(2,1)S(1)} %collective-permute-done), kind=kLoop, calls=%fused_computation | loop fusion | flops 3145728 | bytes 8388608 | tf_op jit(solution)/shard_map/convert_element_type | solution.py:444
  (14 shorter events, 0.5 us)
Async XLA Ops:
  99.4 2.2 %copy-start = (bf16[4,1,2,512,512]{4,3,2,1,0:T(8,128)(2,1)S(1)}, bf16[4,1,2,512,512]{4,3,2,1,0:T(8,128)(2,1)}, u32[]{:S(2)}) copy-start(bf16[4,1,2,512,512]{4,3,2,1,0:T(8,128)(2,1)} %param.8) | copy-start | bytes 12582916
  101.6 2.2 %copy-start.1 = (bf16[4,8,256,256]{3,2,1,0:T(8,128)(2,1)S(1)}, bf16[4,8,256,256]{3,2,1,0:T(8,128)(2,1)}, u32[]{:S(2)}) copy-start(bf16[4,8,256,256]{3,2,1,0:T(8,128)(2,1)} %get-tuple-element.12) | copy-start | bytes 12582916
  103.8 0.7 copy-start.2
  104.5 0.7 copy-start.3
  111.8 29.9 %collective-permute-start = (bf16[8,256,512]{2,1,0:T(8,128)(2,1)S(1)}, bf16[8,256,512]{2,1,0:T(8,128)(2,1)S(1)}, u32[]{:S(2)}, u32[]{:S(2)}) collective-permute-start(bf16[8,256,512]{2,1,0:T(8,128)(2,1)S(1)} %terms_up.1), channel_id=1, source_target_pairs={{0,8},{8,16},{16,24},{1,9},{9,17},{17,25},{2,10},{10,18},{18,26},{... | collective-permute-start | bytes 6291464 | tf_op jit(solution)/shard_map/ppermute | solution.py:442

commit v6 on v5

--- a/solution.py
+++ b/solution.py
@@ -277,7 +277,7 @@
                             @pl.when(carried(k + 1, way, b, sources[way]))
                             def _():
                                 block_copy(k + 1, way, b, sources[way]).start()
-        if staged and k == half // 2:
+        if staged and k == 1:
             for inner, edge in ((1, 0), (sec_a - 2, sec_a - 1)):
                 @pl.when(a == inner)
                 def _(edge=edge):

time: 147 us -> 162 us (1.10); the launches traced: 144 us -> 161 us
  Pallas kernels: 108 us -> 129 us
  starting transfers between devices: 22.4 us -> 2.77 us
  waiting for transfers between devices: 0.01 us -> 15.7 us
    ppermute x1, starting transfers between devices: 22.4 us -> 2.77 us  [body(): up = lax.ppermute(up, 'sec', [(k, k + 1) for k in range(sec_a - 1)])]
    pallas_call x1, Pallas kernels: 93.8 us -> 112 us  [gather(): pl.pallas_call(functools.partial(gather_kernel, n, chans, sec_a, sec_b),...]
    ppermute x1, waiting for transfers between devices: 0.01 us -> 15.7 us  [body(): up = lax.ppermute(up, 'sec', [(k, k + 1) for k in range(sec_a - 1)])]
    pallas_call x2, Pallas kernels: 14.1 us -> 17.3 us  [terms(): pl.pallas_call(functools.partial(terms_kernel, up_a, up_a * chans + at, c...]
  transfers between devices with their start and end apart: 1 -> 1, of which waited for: 0 -> 1; matrix products, arithmetic and copies ran while one was open for 0% -> 0% of each run, Pallas kernels for 5% -> 6%
where the time goes in v6:
time: 162 us; the launch traced here: 161 us
  Pallas kernels  129 us (80%)
  waiting for transfers between devices  15.7 us (10%)
  local copies, waits for them, and re-layouts  9.79 us (6%)
  other arithmetic  3.69 us (2%)
  starting transfers between devices  2.77 us (2%)
    pallas_call x1, Pallas kernels, gather(): pl.pallas_call(functools.partial(gather_kernel, n, chans, sec_a, sec_b),...  112 us
    pallas_call x2, Pallas kernels, terms(): pl.pallas_call(functools.partial(terms_kernel, up_a, up_a * chans + at, c...  17.3 us
    ppermute x1, waiting for transfers between devices, body(): up = lax.ppermute(up, 'sec', [(k, k + 1) for k in range(sec_a - 1)])  15.7 us
    unnamed x10, local copies, waits for them, and re-layouts  7.26 us
  transfers between devices with their start and end apart: 1, of which 1 were waited for; matrix products, arithmetic and copies ran while one was open for 0% of the time, Pallas kernels for 6%

profile of v6, /device:TPU:30, one launch (start us, length us, event | category | flops | bytes accessed | tf_op | source)
XLA Modules:
  0.0 161.2 jit_solution(1256950622277277411)
XLA Ops:
  0.0 0.8 reshape.116
  0.9 0.1 add.152
  1.0 0.1 add.157
  1.2 0.1 add.160
  1.3 0.8 copy.12
  2.0 0.1 reshape.111.ksz
  2.1 0.8 copy.11
  2.9 0.7 reshape.107.sizes
  3.5 0.7 slice_multiply_fusion
  4.3 0.1 mul.70
  4.4 0.1 rem.47
  4.4 0.1 div.21
  4.8 0.1 fusion.1
  4.9 0.7 fusion.info
  5.7 112.0 %gather_row.1 = (bf16[64,256,512]{2,1,0:T(8,128)(2,1)}, bf16[4,8,256,256]{3,2,1,0:T(8,128)(2,1)}, f32[8,72,128]{2,1,0:T(8,128)}, s32[8,128]{1,0:T(8,128)}, f32[8,128]{1,0:T(8,128)}) custom-call(s32[8]{0:T(128)} %reshape.107.sizes, bf16[8,256,512]{2,1,0:T(8,128)(2,1)} %bitcast.22, bf16[8,256,256]{2,1,0:T(8,128)(2,1)} %bitcast.23, f32[72,128]{1,0:T(8,128)} %fusion.info), custom_call_target="tpu_custom_call" | custom-call | tf_op jit(solution)/shard_map/gather_row/pallas_call | solution.py:313
  117.7 2.2 %copy-done = bf16[4,1,2,512,512]{4,3,2,1,0:T(8,128)(2,1)S(1)} copy-done((bf16[4,1,2,512,512]{4,3,2,1,0:T(8,128)(2,1)S(1)}, bf16[4,1,2,512,512]{4,3,2,1,0:T(8,128)(2,1)}, u32[]{:S(2)}) %copy-start) | copy-done | bytes 4194328
  119.8 2.2 %copy-done.1 = bf16[4,8,256,256]{3,2,1,0:T(8,128)(2,1)S(1)} copy-done((bf16[4,8,256,256]{3,2,1,0:T(8,128)(2,1)S(1)}, bf16[4,8,256,256]{3,2,1,0:T(8,128)(2,1)}, u32[]{:S(2)}) %copy-start.1) | copy-done | bytes 4194328
  122.0 0.7 copy-done.2
  122.7 0.7 copy-done.3
  123.4 8.4 %terms_up.1 = bf16[8,256,512]{2,1,0:T(8,128)(2,1)S(1)} custom-call(s32[8,128]{1,0:T(8,128)S(1)} %copy-done.2, f32[8,128]{1,0:T(8,128)S(1)} %copy-done.3, s32[8]{0:T(128)S(1)} %reshape.111.ksz, bf16[64,256,512]{2,1,0:T(8,128)(2,1)} %get-tuple-element.11.env, bf16[32,256,256]{2,1,0:T(8,128)(2,1)S(1)} %bitcast.20, bf16[8,512,512]{2,1,0:T(8,128)(2,1)S(1)} %bitcast.18), custom_call_target="tpu_custom_call" | custom-call | flops 5000000000 | bytes 16777216 | tf_op jit(solution)/shard_map/terms_up/pallas_call | solution.py:397
  131.8 2.8 %collective-permute-start = (bf16[8,256,512]{2,1,0:T(8,128)(2,1)S(1)}, bf16[8,256,512]{2,1,0:T(8,128)(2,1)S(1)}, u32[]{:S(2)}, u32[]{:S(2)}) collective-permute-start(bf16[8,256,512]{2,1,0:T(8,128)(2,1)S(1)} %terms_up.1), channel_id=1, source_target_pairs={{0,8},{8,16},{16,24},{1,9},{9,17},{17,25},{2,10},{10,18},{18,26},{... | collective-permute-start | bytes 6291464 | tf_op jit(solution)/shard_map/ppermute | solution.py:442
  134.5 8.9 %terms_same.1 = f32[8,256,512]{2,1,0:T(8,128)S(1)} custom-call(s32[8,128]{1,0:T(8,128)S(1)} %copy-done.2, f32[8,128]{1,0:T(8,128)S(1)} %copy-done.3, s32[8]{0:T(128)S(1)} %reshape.111.ksz, bf16[64,256,512]{2,1,0:T(8,128)(2,1)} %get-tuple-element.11.env, bf16[32,256,256]{2,1,0:T(8,128)(2,1)S(1)} %bitcast.21, bf16[8,512,512]{2,1,0:T(8,128)(2,1)S(1)} %bitcast.19), custom_call_target="tpu_custom_call" | custom-call | flops 5000000000 | bytes 16777216 | tf_op jit(solution)/shard_map/terms_same/pallas_call | solution.py:397
  143.4 15.7 %collective-permute-done = bf16[8,256,512]{2,1,0:T(8,128)(2,1)S(1)} collective-permute-done((bf16[8,256,512]{2,1,0:T(8,128)(2,1)S(1)}, bf16[8,256,512]{2,1,0:T(8,128)(2,1)S(1)}, u32[]{:S(2)}, u32[]{:S(2)}) %collective-permute-start) | collective-permute-done | bytes 2097184 | tf_op jit(solution)/shard_map/ppermute | solution.py:442
  159.1 2.1 %add_convert_fusion = bf16[8,256,512]{2,1,0:T(8,128)(2,1)} fusion(f32[8,256,512]{2,1,0:T(8,128)S(1)} %terms_same.1, bf16[8,256,512]{2,1,0:T(8,128)(2,1)S(1)} %collective-permute-done), kind=kLoop, calls=%fused_computation | loop fusion | flops 3145728 | bytes 8388608 | tf_op jit(solution)/shard_map/convert_element_type | solution.py:444
  (14 shorter events, 0.6 us)
Async XLA Ops:
  117.7 2.2 %copy-start = (bf16[4,1,2,512,512]{4,3,2,1,0:T(8,128)(2,1)S(1)}, bf16[4,1,2,512,512]{4,3,2,1,0:T(8,128)(2,1)}, u32[]{:S(2)}) copy-start(bf16[4,1,2,512,512]{4,3,2,1,0:T(8,128)(2,1)} %param.8) | copy-start | bytes 12582916
  119.8 2.2 %copy-start.1 = (bf16[4,8,256,256]{3,2,1,0:T(8,128)(2,1)S(1)}, bf16[4,8,256,256]{3,2,1,0:T(8,128)(2,1)}, u32[]{:S(2)}) copy-start(bf16[4,8,256,256]{3,2,1,0:T(8,128)(2,1)} %get-tuple-element.12) | copy-start | bytes 12582916
  122.0 0.7 copy-start.2
  122.7 0.7 copy-start.3
  131.8 27.4 %collective-permute-start = (bf16[8,256,512]{2,1,0:T(8,128)(2,1)S(1)}, bf16[8,256,512]{2,1,0:T(8,128)(2,1)S(1)}, u32[]{:S(2)}, u32[]{:S(2)}) collective-permute-start(bf16[8,256,512]{2,1,0:T(8,128)(2,1)S(1)} %terms_up.1), channel_id=1, source_target_pairs={{0,8},{8,16},{16,24},{1,9},{9,17},{17,25},{2,10},{10,18},{18,26},{... | collective-permute-start | bytes 6291464 | tf_op jit(solution)/shard_map/ppermute | solution.py:442

commit v7 on v6

--- a/solution.py
+++ b/solution.py
@@ -277,7 +277,7 @@
                             @pl.when(carried(k + 1, way, b, sources[way]))
                             def _():
                                 block_copy(k + 1, way, b, sources[way]).start()
-        if staged and k == 1:
+        if staged and k == half // 2 + 1:
             for inner, edge in ((1, 0), (sec_a - 2, sec_a - 1)):
                 @pl.when(a == inner)
                 def _(edge=edge):

time: 162 us -> 148 us (0.914)
  starting transfers between devices: 2.77 us -> 38.8 us
  Pallas kernels: 129 us -> 94.2 us
  waiting for transfers between devices: 15.7 us -> 0.01 us
    ppermute x1, starting transfers between devices: 2.77 us -> 38.8 us  [body(): up = lax.ppermute(up, 'sec', [(k, k + 1) for k in range(sec_a - 1)])]
    pallas_call x1, Pallas kernels: 112 us -> 80 us  [gather(): pl.pallas_call(functools.partial(gather_kernel, n, chans, sec_a, sec_b),...]
    ppermute x1, waiting for transfers between devices: 15.7 us -> 0.01 us  [body(): up = lax.ppermute(up, 'sec', [(k, k + 1) for k in range(sec_a - 1)])]
    pallas_call x2, Pallas kernels: 17.3 us -> 14.2 us  [terms(): pl.pallas_call(functools.partial(terms_kernel, up_a, up_a * chans + at, c...]
  transfers between devices with their start and end apart: 1 -> 1, of which waited for: 1 -> 0; matrix products, arithmetic and copies ran while one was open for 0% -> 0% of each run, Pallas kernels for 6% -> 7%
where the time goes in v7:
time: 148 us; the launch traced here: 147 us
  Pallas kernels  94.2 us (64%)
  starting transfers between devices  38.8 us (26%)
  local copies, waits for them, and re-layouts  9.79 us (7%)
  other arithmetic  3.7 us (2%)
    pallas_call x1, Pallas kernels, gather(): pl.pallas_call(functools.partial(gather_kernel, n, chans, sec_a, sec_b),...  80 us
    ppermute x1, starting transfers between devices, body(): up = lax.ppermute(up, 'sec', [(k, k + 1) for k in range(sec_a - 1)])  38.8 us
    pallas_call x2, Pallas kernels, terms(): pl.pallas_call(functools.partial(terms_kernel, up_a, up_a * chans + at, c...  14.2 us
    unnamed x10, local copies, waits for them, and re-layouts  7.26 us
  transfers between devices with their start and end apart: 1, of which 0 were waited for; matrix products, arithmetic and copies ran while one was open for 0% of the time, Pallas kernels for 7%

profile of v7, /device:TPU:30, one launch (start us, length us, event | category | flops | bytes accessed | tf_op | source)
XLA Modules:
  0.0 146.5 jit_solution(15103927255181277626)
XLA Ops:
  0.0 0.8 reshape.116
  0.9 0.1 add.152
  1.0 0.1 add.157
  1.2 0.1 add.160
  1.3 0.8 copy.12
  2.0 0.1 reshape.111.ksz
  2.1 0.8 copy.11
  2.9 0.7 reshape.107.sizes
  3.5 0.7 slice_multiply_fusion
  4.3 0.1 mul.70
  4.4 0.1 rem.47
  4.4 0.1 div.21
  4.5 0.1 squeeze.9
  4.8 0.1 fusion.1
  4.9 0.7 fusion.info
  5.7 80.0 %gather_row.1 = (bf16[64,256,512]{2,1,0:T(8,128)(2,1)}, bf16[4,8,256,256]{3,2,1,0:T(8,128)(2,1)}, f32[8,72,128]{2,1,0:T(8,128)}, s32[8,128]{1,0:T(8,128)}, f32[8,128]{1,0:T(8,128)}) custom-call(s32[8]{0:T(128)} %reshape.107.sizes, bf16[8,256,512]{2,1,0:T(8,128)(2,1)} %bitcast.22, bf16[8,256,256]{2,1,0:T(8,128)(2,1)} %bitcast.23, f32[72,128]{1,0:T(8,128)} %fusion.info), custom_call_target="tpu_custom_call" | custom-call | tf_op jit(solution)/shard_map/gather_row/pallas_call | solution.py:313
  85.7 2.2 %copy-done = bf16[4,1,2,512,512]{4,3,2,1,0:T(8,128)(2,1)S(1)} copy-done((bf16[4,1,2,512,512]{4,3,2,1,0:T(8,128)(2,1)S(1)}, bf16[4,1,2,512,512]{4,3,2,1,0:T(8,128)(2,1)}, u32[]{:S(2)}) %copy-start) | copy-done | bytes 4194328
  87.8 2.2 %copy-done.1 = bf16[4,8,256,256]{3,2,1,0:T(8,128)(2,1)S(1)} copy-done((bf16[4,8,256,256]{3,2,1,0:T(8,128)(2,1)S(1)}, bf16[4,8,256,256]{3,2,1,0:T(8,128)(2,1)}, u32[]{:S(2)}) %copy-start.1) | copy-done | bytes 4194328
  90.0 0.7 copy-done.2
  90.7 0.7 copy-done.3
  91.4 4.2 %terms_up.1 = bf16[8,256,512]{2,1,0:T(8,128)(2,1)S(1)} custom-call(s32[8,128]{1,0:T(8,128)S(1)} %copy-done.2, f32[8,128]{1,0:T(8,128)S(1)} %copy-done.3, s32[8]{0:T(128)S(1)} %reshape.111.ksz, bf16[64,256,512]{2,1,0:T(8,128)(2,1)} %get-tuple-element.11.env, bf16[32,256,256]{2,1,0:T(8,128)(2,1)S(1)} %bitcast.20, bf16[8,512,512]{2,1,0:T(8,128)(2,1)S(1)} %bitcast.18), custom_call_target="tpu_custom_call" | custom-call | flops 5000000000 | bytes 16777216 | tf_op jit(solution)/shard_map/terms_up/pallas_call | solution.py:397
  95.6 38.8 %collective-permute-start = (bf16[8,256,512]{2,1,0:T(8,128)(2,1)S(1)}, bf16[8,256,512]{2,1,0:T(8,128)(2,1)S(1)}, u32[]{:S(2)}, u32[]{:S(2)}) collective-permute-start(bf16[8,256,512]{2,1,0:T(8,128)(2,1)S(1)} %terms_up.1), channel_id=1, source_target_pairs={{0,8},{8,16},{16,24},{1,9},{9,17},{17,25},{2,10},{10,18},{18,26},{... | collective-permute-start | bytes 6291464 | tf_op jit(solution)/shard_map/ppermute | solution.py:442
  134.4 10.0 %terms_same.1 = f32[8,256,512]{2,1,0:T(8,128)S(1)} custom-call(s32[8,128]{1,0:T(8,128)S(1)} %copy-done.2, f32[8,128]{1,0:T(8,128)S(1)} %copy-done.3, s32[8]{0:T(128)S(1)} %reshape.111.ksz, bf16[64,256,512]{2,1,0:T(8,128)(2,1)} %get-tuple-element.11.env, bf16[32,256,256]{2,1,0:T(8,128)(2,1)S(1)} %bitcast.21, bf16[8,512,512]{2,1,0:T(8,128)(2,1)S(1)} %bitcast.19), custom_call_target="tpu_custom_call" | custom-call | flops 5000000000 | bytes 16777216 | tf_op jit(solution)/shard_map/terms_same/pallas_call | solution.py:397
  144.4 2.1 %add_convert_fusion = bf16[8,256,512]{2,1,0:T(8,128)(2,1)} fusion(f32[8,256,512]{2,1,0:T(8,128)S(1)} %terms_same.1, bf16[8,256,512]{2,1,0:T(8,128)(2,1)S(1)} %collective-permute-done), kind=kLoop, calls=%fused_computation | loop fusion | flops 3145728 | bytes 8388608 | tf_op jit(solution)/shard_map/convert_element_type | solution.py:444
  (14 shorter events, 0.5 us)
Async XLA Ops:
  85.6 2.2 %copy-start = (bf16[4,1,2,512,512]{4,3,2,1,0:T(8,128)(2,1)S(1)}, bf16[4,1,2,512,512]{4,3,2,1,0:T(8,128)(2,1)}, u32[]{:S(2)}) copy-start(bf16[4,1,2,512,512]{4,3,2,1,0:T(8,128)(2,1)} %param.8) | copy-start | bytes 12582916
  87.8 2.2 %copy-start.1 = (bf16[4,8,256,256]{3,2,1,0:T(8,128)(2,1)S(1)}, bf16[4,8,256,256]{3,2,1,0:T(8,128)(2,1)}, u32[]{:S(2)}) copy-start(bf16[4,8,256,256]{3,2,1,0:T(8,128)(2,1)} %get-tuple-element.12) | copy-start | bytes 12582916
  90.0 0.7 copy-start.2
  90.7 0.7 copy-start.3
  95.6 48.8 %collective-permute-start = (bf16[8,256,512]{2,1,0:T(8,128)(2,1)S(1)}, bf16[8,256,512]{2,1,0:T(8,128)(2,1)S(1)}, u32[]{:S(2)}, u32[]{:S(2)}) collective-permute-start(bf16[8,256,512]{2,1,0:T(8,128)(2,1)S(1)} %terms_up.1), channel_id=1, source_target_pairs={{0,8},{8,16},{16,24},{1,9},{9,17},{17,25},{2,10},{10,18},{18,26},{... | collective-permute-start | bytes 6291464 | tf_op jit(solution)/shard_map/ppermute | solution.py:442
